TPU v7x, 256 devices: a whole 4x4x8 slice. The times are simulated.
256 devices in a mesh: seq: 8 (over x, core), batch: 32 (over z, y).
Axes of the slice: x: 4, y: 4, z: 8, core: 2. Of those that a mesh axis runs over, the one named last changes fastest.
Arguments:
- patches: bfloat16 [32, 2560, 1280], P('batch', 'seq'), may hold values from -30 to 30
- window_ids: int32 [32, 640], P('batch', 'seq'), may hold values from 0 to 79, never falling along the last dimension, each value on 1 to 16 neighbouring positions
- norm_gain: float32 [1280], replicated, may hold values from 0.1 to 1.9
- w_qkv: bfloat16 [3, 1280, 1280], P(None, None, 'seq'), may hold values from -2 to 2
- b_qkv: float32 [3, 1280], replicated, may hold values from -3 to 3
- w_proj: bfloat16 [1280, 1280], P('seq'), may hold values from -0.15625 to 0.15625
- b_proj: float32 [1280], replicated, may hold values from -3 to 3
- merge_gain: float32 [1280], replicated, may hold values from 0.1 to 1.9
- token_lists: int32 [20480], replicated, may hold values from 0 to 20479, as said below
- req_owner: int32 [128], replicated, may hold values from 0 to 31, as said below
- req_counts: int32 [128], replicated, may hold values from 1 to 319, as said below
Outputs:
- cache: bfloat16 [32, 1276, 5120], P('batch', None, 'seq')
Inputs may be any that keep to these rules, and one draw needn't show every extreme that they name: `token_lists`: a permutation of the merged tokens; the merged tokens of one group that fall in one owner's requests number at most 40. `req_owner`: each owner holds exactly 4 requests. `req_counts`: they sum to 20480.
All inputs are finite; a program needn't handle non-finite values.
Results may differ from a plain program's by a relative error of at most 0.005.
Values may be sent and summed in bfloat16 or wider, within the bound.
A program may use at most 128 MiB of HBM per device.

v0:
```python
import math

import jax
import jax.numpy as jnp
from jax import lax
from jax.sharding import PartitionSpec as P

HEADS = 16
REQS = 4
HALO = 63


def rms_scaled(values, gain):
    return values * lax.rsqrt(jnp.mean(values * values, axis=-1, keepdims=True) + 1e-06) * gain


def band_attend(queries, keys_band, values_band, query_ids, key_ids, margin):
    row_count = queries.shape[0]
    block_rows = min(512, row_count)
    block_count = row_count // block_rows
    band_width = block_rows + 2 * margin
    scaling = 1.0 / math.sqrt(queries.shape[2])

    def one_block(block_index):
        starting = block_index * block_rows
        query_block = lax.dynamic_slice_in_dim(queries, starting, block_rows, 0)
        key_block = lax.dynamic_slice_in_dim(keys_band, starting, band_width, 0)
        value_block = lax.dynamic_slice_in_dim(values_band, starting, band_width, 0)
        own_ids = lax.dynamic_slice_in_dim(query_ids, starting, block_rows, 0)
        other_ids = lax.dynamic_slice_in_dim(key_ids, starting, band_width, 0)
        matches = own_ids[:, None] == other_ids[None, :]
        scores = (
            jnp.einsum("qhd,khd->hqk", query_block, key_block, preferred_element_type=jnp.float32)
            * scaling
        )
        scores = jnp.where(matches[None], scores, -1e30)
        maxima = jnp.max(scores, axis=2, keepdims=True)
        exponent = jnp.exp(scores - maxima)
        weights = (exponent / jnp.sum(exponent, axis=2, keepdims=True)).astype(jnp.bfloat16)
        mixed = jnp.einsum("hqk,khd->qhd", weights, value_block, preferred_element_type=jnp.float32)
        return mixed.astype(jnp.bfloat16)

    attended = lax.map(one_block, jnp.arange(block_count, dtype=jnp.int32))
    return attended.reshape(row_count, -1)


def attend_sequence(qkv_rows, head_count, padded_ids, query_ids):
    row_count = qkv_rows.shape[0]
    head_size = qkv_rows.shape[2] // head_count
    widths = ((HALO, HALO), (0, 0), (0, 0))
    queries = qkv_rows[:, 0].reshape(row_count, head_count, head_size)
    keys_band = jnp.pad(qkv_rows[:, 1].reshape(row_count, head_count, head_size), widths)
    values_band = jnp.pad(qkv_rows[:, 2].reshape(row_count, head_count, head_size), widths)
    return band_attend(queries, keys_band, values_band, query_ids, padded_ids, HALO)


def slot_tables(token_lists, req_owner, req_counts, slot_size):
    total_slots = token_lists.shape[0]
    request_total = req_counts.shape[0]
    ends = jnp.cumsum(req_counts)
    starts = ends - req_counts
    slots = jnp.arange(total_slots, dtype=jnp.int32)
    inside = (slots[:, None] >= starts[None, :]) & (slots[:, None] < ends[None, :])
    requests = jnp.arange(request_total, dtype=jnp.int32)
    same_owner = req_owner[None, :] == req_owner[:, None]
    ranks = jnp.sum(same_owner & (requests[None, :] < requests[:, None]), axis=1)
    slot_owner = jnp.sum(jnp.where(inside, req_owner[None, :], 0), axis=1)
    slot_row = jnp.sum(jnp.where(inside, (ranks * slot_size - starts)[None, :], 0), axis=1) + slots
    return (slot_owner, slot_row)


def shards(
    patches,
    window_ids,
    norm_gain,
    w_qkv,
    b_qkv,
    w_proj,
    b_proj,
    merge_gain,
    token_lists,
    req_owner,
    req_counts,
):
    seq_count = lax.axis_size("seq")
    batch_place = lax.axis_index("batch")
    patch_rows = patches[0]
    rows_here = patch_rows.shape[0]
    width = patch_rows.shape[1]
    rows_float = patch_rows.astype(jnp.float32)
    normalized = rms_scaled(rows_float, norm_gain).astype(jnp.bfloat16)
    unit_ids = lax.all_gather(window_ids, "seq", axis=1, tiled=True)[0]
    group_ids = jnp.repeat(unit_ids, 4)
    padded_ids = jnp.pad(group_ids, (HALO, HALO), constant_values=-1)
    product = jnp.einsum(
        "rw,iwc->ric",
        normalized,
        lax.all_gather(w_qkv, "seq", axis=2, tiled=True),
        preferred_element_type=jnp.float32,
    )
    qkv_own = (product + b_qkv[None]).astype(jnp.bfloat16)
    qkv_group = lax.all_to_all(qkv_own, "seq", split_axis=2, concat_axis=0, tiled=True)
    attended_local = attend_sequence(qkv_group, HEADS // seq_count, padded_ids, group_ids)
    attended_own = lax.all_to_all(attended_local, "seq", split_axis=0, concat_axis=1, tiled=True)
    projected = jnp.dot(
        attended_own,
        lax.all_gather(w_proj, "seq", axis=0, tiled=True),
        preferred_element_type=jnp.float32,
    )
    resid = rows_float + projected + b_proj
    normed = rms_scaled(resid, merge_gain)
    merged = normed.reshape(rows_here // 4, 4 * width).astype(jnp.bfloat16)
    grouped = lax.all_to_all(merged, "seq", split_axis=1, concat_axis=0, tiled=True)
    group_size = grouped.shape[0]
    feature_cols = grouped.shape[1]
    slot_size = 2 * (group_size // REQS) - 1
    capacity = REQS * slot_size
    slot_owner, slot_row = slot_tables(token_lists, req_owner, req_counts, slot_size)
    mine = slot_owner == batch_place
    sources = (
        jnp.full((capacity + 1,), -1, jnp.int32)
        .at[jnp.where(mine, slot_row, capacity)]
        .set(token_lists)[:capacity]
    )
    blank = jnp.zeros((capacity, feature_cols), jnp.bfloat16)
    group_piece = lax.all_gather(grouped, "batch", axis=0, tiled=True)
    present = (sources >= 0) & (sources < group_piece.shape[0])
    chosen = jnp.take(group_piece, jnp.clip(sources, 0, group_piece.shape[0] - 1), axis=0)
    cache_rows = jnp.where(present[:, None], chosen, blank)
    return cache_rows[None]


def solution(mesh):
    return jax.shard_map(
        shards,
        mesh=mesh,
        in_specs=(
            P("batch", "seq", None),
            P("batch", "seq"),
            P(),
            P(None, None, "seq"),
            P(),
            P("seq", None),
            P(),
            P(),
            P(),
            P(),
            P(),
        ),
        out_specs=P("batch", None, "seq"),
        check_vma=False,
    )
```

profile of v0, /device:TPU:27, one launch (start us, length us, event | category | flops | bytes accessed | tf_op | source)
XLA Modules:
  0.0 448.7 jit_solution(11778636744475135428)
XLA Ops:
  6.5 0.7 all-gather.4.cloned.1.call-update
  7.3 1.4 fusion.44
  8.7 61.2 %all-gather.4.cloned.1.call-done = bf16[3,1280,1280]{1,2,0:T(8,128)(2,1)} async-done(((bf16[3,1280,160]{1,2,0:T(8,128)(2,1)}), bf16[3,1280,1280]{1,2,0:T(8,128)(2,1)}) %all-gather.4.cloned.1.call-update) | async-done | bytes 9830416 | tf_op jit(solution)/shard_map/all_gather | solution.py:98
  69.9 7.5 %add_convert_fusion = bf16[320,3,1280]{2,0,1:T(8,128)(2,1)S(1)} fusion(bf16[3,1280,1280]{1,2,0:T(8,128)(2,1)} %all-gather.4.cloned.1.call-done, f32[3,1280]{1,0:T(4,128)} %param.17, bf16[1,320,1280]{2,1,0:T(8,128)(2,1)} %param.13, f32[1280]{0:T(1024)} %param.15, f32[320]{0:T(512)S(1)} %add_rsqrt_fusion.1), kind=kOutput, calls=%fused_computation.35 | convolution fusion | flops 3149824000 | bytes 13128960 | tf_op jit(solution)/shard_map/rw,iwc->ric/dot_general | solution.py:95
  77.4 6.2 %copy.28 = bf16[320,3,1280]{0,1,2:T(4,128)(2,1)} copy(bf16[320,3,1280]{2,0,1:T(8,128)(2,1)S(1)} %add_convert_fusion) | data formatting | bytes 4915200 | tf_op jit(solution)/shard_map/convert_element_type | solution.py:101
  83.7 5.7 %all-to-all-start = ((bf16[320,3,1280]{0,1,2:T(4,128)(2,1)}), bf16[320,3,1280]{0,1,2:T(4,128)(2,1)}, u32[]{:S(2)}, u32[]{:S(2)}) async-start(bf16[320,3,1280]{0,1,2:T(4,128)(2,1)} %copy.28), calls=%async_computation | async-start | bytes 7864320 | tf_op jit(solution)/shard_map/all_to_all | solution.py:102
  89.4 0.7 all-gather.6.cloned.1.call-update
  90.1 0.6 dynamic-slice
  91.6 57.6 %all-reduce.3 = s32[640]{0:T(1024)S(1)} all-reduce(s32[640]{0:T(1024)S(1)} %bitcast_dynamic-update-slice_fusion), channel_id=1, replica_groups=mesh['seq'=8,'batch'=32] {'seq'}, use_global_device_ids=true, to_apply=%add.3 | all-reduce | flops 640 | bytes 5120
  149.7 2.5 copy.29
  152.2 1.1 copy.30
  153.3 3.5 all_to_all.42
  156.8 1.8 fusion.61
  158.6 0.3 pad.13
  158.9 0.3 pad.11
  159.3 31.6 %while.10 = (s32[]{:T(128)}, bf16[5,512,2,80]{1,3,2,0:T(8,128)(2,1)}, s32[5]{0:T(128)S(1)}, bf16[2686,2,80]{0,2,1:T(8,128)(2,1)S(1)}, s32[2560]{0:T(1024)S(1)}, ...) while((s32[]{:T(128)}, ...), condition=%wide.region_9.10_spmd, body=%wide.region_6.9_spmd.sunk | while | flops 319880448 | bytes 2112208 | solution.py:43
  159.3 0.7 dynamic_slice.58
  160.8 0.3 broadcast_compare_fusion.3
  161.1 1.4 fusion.77
  162.4 3.2 fusion.78
  165.6 0.7 dynamic_slice.58
  167.1 0.3 broadcast_compare_fusion.3
  167.4 1.4 fusion.77
  168.8 3.2 fusion.78
  171.9 0.7 dynamic_slice.58
  173.4 0.3 broadcast_compare_fusion.3
  173.7 1.4 fusion.77
  175.1 3.2 fusion.78
  178.3 0.7 dynamic_slice.58
  179.8 0.3 broadcast_compare_fusion.3
  180.0 1.4 fusion.77
  181.4 3.2 fusion.78
  184.6 0.7 dynamic_slice.58
  186.3 1.4 fusion.77
  187.7 3.2 fusion.78
  190.9 1.6 copy.31
  192.5 1.3 all_to_all.43
  193.9 1.1 copy.32
  194.9 6.5 %all-to-all-start.1 = ((bf16[8,320,160]{1,2,0:T(8,128)(2,1)}), bf16[8,320,160]{1,2,0:T(8,128)(2,1)S(1)}, u32[]{:S(2)}, u32[]{:S(2)}) async-start(bf16[8,320,160]{1,2,0:T(8,128)(2,1)} %copy.32), calls=%async_computation.1 | async-start | bytes 1966080 | tf_op jit(solution)/shard_map/all_to_all | solution.py:104
  201.5 13.3 %all-to-all-done.1 = bf16[8,320,160]{1,2,0:T(8,128)(2,1)S(1)} async-done(((bf16[8,320,160]{1,2,0:T(8,128)(2,1)}), bf16[8,320,160]{1,2,0:T(8,128)(2,1)S(1)}, u32[]{:S(2)}, u32[]{:S(2)}) %all-to-all-start.1) | async-done | bytes 819232 | tf_op jit(solution)/shard_map/all_to_all | solution.py:104
  214.8 3.4 multiply_reduce_fusion
  218.4 0.3 convert_element_type.40
  218.8 17.0 %all_to_all.53 = bf16[80,8,640]{2,0,1:T(8,128)(2,1)} all-to-all(bf16[80,8,640]{2,0,1:T(8,128)(2,1)S(1)} %copy.33), channel_id=1, replica_groups=mesh['seq'=8,'batch'=32] {'seq'}, dimensions={1} | all-to-all | bytes 1638400 | tf_op jit(solution)/shard_map/all_to_all | solution.py:113
  236.4 6.1 %select_reduce_fusion = (s32[20480]{0:T(1024)S(1)}, s32[20480]{0:T(1024)S(1)}) fusion(s32[128]{0:T(128)S(1)} %get-tuple-element.66, s32[128]{0:T(128)S(1)} %reduce, s32[128]{0:T(128)S(1)} %get-tuple-element.67, s32[128]{0:T(128)S(1)} %copy-done.3), kind=kLoop, calls=%fused_computation.30 | loop fusion | flops 18309120 | bytes 165888 | tf_op jit(solution)/shard_map/reduce_sum | solution.py:68
  242.8 75.5 %scatter_custom_fusion = s32[1277]{0:T(1024)S(1)} fusion(s32[20480]{0:T(1024)S(1)} %bitcast.61, s32[20480]{0:T(1024)} %param.21, s32[]{:T(128)} %constant.18.clone.1), kind=kCustom, calls=%fused_computation.61 | custom fusion | bytes 5620 | tf_op jit(solution)/shard_map/scatter | solution.py:123
  318.3 105.6 %all-gather.8.cloned.1.call-done = bf16[20480,640]{1,0:T(8,128)(2,1)} async-done(((bf16[640,640]{1,0:T(8,128)(2,1)}), bf16[20480,640]{1,0:T(8,128)(2,1)}) %all-gather.8.cloned.1.call-update) | async-done | bytes 26214416 | tf_op jit(solution)/shard_map/all_gather | solution.py:126
  423.9 16.3 %gather_fusion = bf16[1276,640]{1,0:T(8,128)(2,1)S(1)} fusion(bf16[20480,640]{1,0:T(8,128)(2,1)} %all-gather.8.cloned.1.call-done, s32[2048]{0:T(1024)S(1)} %pad_clamp_fusion), kind=kCustom, calls=%fused_computation | custom fusion | bytes 3271664 | tf_op jit(solution)/shard_map/jit(_take)/gather | solution.py:128
  440.3 1.9 fusion.47
  (52 shorter events, 2.7 us)
Async XLA Ops:
  6.5 63.4 %all-gather.4.cloned.1.call-start = ((), (), s32[]{:S(2)}) async-start(), calls=%async_computation.3 | async-start | bytes 11059200 | tf_op jit(solution)/shard_map/all_gather | solution.py:98
  83.7 6.5 %copy-start.6 = (u32[256]{0:T(256)S(1)}, u32[256]{0:T(256)}, u32[]{:S(2)}) copy-start(u32[256]{0:T(256)} %constant.82) | copy-start | bytes 3076
  83.7 7.8 %copy-start.5 = (s32[1,80]{1,0:T(1,128)S(1)}, s32[1,80]{1,0:T(1,128)}, u32[]{:S(2)}) copy-start(s32[1,80]{1,0:T(1,128)} %param.14) | copy-start | bytes 964
  83.7 66.0 %all-to-all-start = ((bf16[320,3,1280]{0,1,2:T(4,128)(2,1)}), bf16[320,3,1280]{0,1,2:T(4,128)(2,1)}, u32[]{:S(2)}, u32[]{:S(2)}) async-start(bf16[320,3,1280]{0,1,2:T(4,128)(2,1)} %copy.28), calls=%async_computation | async-start | bytes 7864320 | tf_op jit(solution)/shard_map/all_to_all | solution.py:102
  89.4 112.1 %all-gather.6.cloned.1.call-start = ((), (), s32[]{:S(2)}) async-start(), calls=%async_computation.4 | async-start | bytes 3686400 | tf_op jit(solution)/shard_map/all_gather | solution.py:107
  192.5 22.3 %copy-start = (bf16[1,320,1280]{2,1,0:T(8,128)(2,1)S(1)}, bf16[1,320,1280]{2,1,0:T(8,128)(2,1)}, u32[]{:S(2)}) copy-start(bf16[1,320,1280]{2,1,0:T(8,128)(2,1)} %param.13) | copy-start | bytes 2457604
  192.5 22.3 %copy-start.4 = (f32[1280]{0:T(1024)S(1)}, f32[1280]{0:T(1024)}, u32[]{:S(2)}) copy-start(f32[1280]{0:T(1024)} %param.19) | copy-start | bytes 15364
  194.9 19.8 %all-to-all-start.1 = ((bf16[8,320,160]{1,2,0:T(8,128)(2,1)}), bf16[8,320,160]{1,2,0:T(8,128)(2,1)S(1)}, u32[]{:S(2)}, u32[]{:S(2)}) async-start(bf16[8,320,160]{1,2,0:T(8,128)(2,1)} %copy.32), calls=%async_computation.1 | async-start | bytes 1966080 | tf_op jit(solution)/shard_map/all_to_all | solution.py:104
  201.5 222.5 %all-gather.8.cloned.1.call-start = ((), (), s32[]{:S(2)}) async-start(), calls=%async_computation.5 | async-start | bytes 27033600 | tf_op jit(solution)/shard_map/all_gather | solution.py:126
  214.8 3.4 copy-start.1
  218.4 17.4 %copy-start.2 = (s32[128]{0:T(128)S(1)}, s32[128]{0:T(128)}, u32[]{:S(2)}) copy-start(s32[128]{0:T(128)} %param.23) | copy-start | bytes 1540
  218.4 17.8 %copy-start.3 = (s32[128]{0:T(128)S(1)}, s32[128]{0:T(128)}, u32[]{:S(2)}) copy-start(s32[128]{0:T(128)} %param.22) | copy-start | bytes 1540
Sparse Core Ops, SparseCore 0:
  9.2 60.6 all-gather.3
  92.0 45.2 all-gather.5
  236.0 187.9 all-gather.7
where the time goes:
time: 452 us; the launch traced here: 449 us
  waiting for transfers between devices  182 us (40%)
  local copies, waits for them, and re-layouts  117 us (26%)
  blocking collectives  74.6 us (17%)
  matrix products  33.6 us (7%)
  between operations  14 us (3%)
  starting transfers between devices  12.2 us (3%)
  other arithmetic  11.6 us (3%)
    all_gather x1, waiting for transfers between devices, shards(): group_piece = lax.all_gather(grouped, 'batch', axis=0, tiled=True)  106 us
    scatter x1, local copies, waits for them, and re-layouts, shards(): sources = jnp.full((capacity + 1,), -1, jnp.int32).at[jnp.where(mine, slo...  75.5 us
    all_gather x1, waiting for transfers between devices, shards(): lax.all_gather(w_qkv, 'seq', axis=2, tiled=True)  61.2 us
    unnamed x1, blocking collectives  57.6 us
    all_to_all x1, blocking collectives, shards(): lax.all_to_all(merged, 'seq', split_axis=1, concat_axis=0, tiled=True)  17 us
    gather x1, local copies, waits for them, and re-layouts, shards(): jnp.take(group_piece, jnp.clip(sources, 0, group_piece.shape[0] - 1), axi...  16.3 us
    dot_general x5, matrix products, one_block(): jnp.einsum('hqk,khd->qhd', weights, value_block, preferred_element_type=j...  15.9 us
    all_to_all x1, waiting for transfers between devices, shards(): lax.all_to_all(attended_local, 'seq', split_axis=0, concat_axis=1, tiled=...  13.3 us
  transfers between devices with their start and end apart: 5, of which 3 were waited for; matrix products, arithmetic and copies ran while one was open for 27% of the time, Pallas kernels for 0%

commit v1 on v0

--- a/solution.py
+++ b/solution.py
@@ -3,11 +3,20 @@
 import jax
 import jax.numpy as jnp
 from jax import lax
+from jax.experimental import pallas as pl
+from jax.experimental.pallas import tpu as pltpu
 from jax.sharding import PartitionSpec as P
 
 HEADS = 16
 REQS = 4
 HALO = 63
+SLOTS = 40
+GROUP = 640
+TOKENS = 20480
+MOST = 319
+CAP = 1276
+ROWS = 1280
+PER = 8
 
 
 def rms_scaled(values, gain):
@@ -54,19 +63,126 @@
     return band_attend(queries, keys_band, values_band, query_ids, padded_ids, HALO)
 
 
-def slot_tables(token_lists, req_owner, req_counts, slot_size):
-    total_slots = token_lists.shape[0]
-    request_total = req_counts.shape[0]
+def routing_tables(token_lists, req_owner, req_counts, group, owner):
     ends = jnp.cumsum(req_counts)
     starts = ends - req_counts
-    slots = jnp.arange(total_slots, dtype=jnp.int32)
+    slots = jnp.arange(TOKENS, dtype=jnp.int32)
     inside = (slots[:, None] >= starts[None, :]) & (slots[:, None] < ends[None, :])
-    requests = jnp.arange(request_total, dtype=jnp.int32)
-    same_owner = req_owner[None, :] == req_owner[:, None]
-    ranks = jnp.sum(same_owner & (requests[None, :] < requests[:, None]), axis=1)
     slot_owner = jnp.sum(jnp.where(inside, req_owner[None, :], 0), axis=1)
-    slot_row = jnp.sum(jnp.where(inside, (ranks * slot_size - starts)[None, :], 0), axis=1) + slots
-    return (slot_owner, slot_row)
+    local = jnp.arange(GROUP, dtype=jnp.int32)
+    owner_of = jnp.sum(
+        jnp.where(token_lists[:, None] == group * GROUP + local[None, :], slot_owner[:, None], 0), axis=0
+    )
+    before = (owner_of[:, None] == owner_of[None, :]) & (local[:, None] < local[None, :])
+    send_slot = owner_of * SLOTS + jnp.sum(before, axis=0, dtype=jnp.int32)
+    requests = jnp.arange(req_owner.shape[0], dtype=jnp.int32)
+    own = req_owner == owner
+    own_rank = jnp.sum(own[:, None] & (requests[:, None] < requests[None, :]), axis=0)
+    padded = jnp.concatenate([token_lists, jnp.zeros((MOST + 1,), jnp.int32)])
+    held = []
+    for rank in range(REQS):
+        chosen = own & (own_rank == rank)
+        start = jnp.sum(jnp.where(chosen, starts, 0))
+        count = jnp.sum(jnp.where(chosen, req_counts, 0))
+        listed = lax.dynamic_slice(padded, (start,), (MOST,))
+        held.append(jnp.where(jnp.arange(MOST) < count, listed, -1))
+    held.append(jnp.full((ROWS - CAP,), -1, jnp.int32))
+    tokens = jnp.concatenate(held)
+    first = (tokens // GROUP) * GROUP
+    earlier = (tokens[:, None] < tokens[None, :]) & (tokens[:, None] >= first[None, :])
+    taken = jnp.sum(earlier, axis=0, dtype=jnp.int32)
+    source = jnp.where(tokens >= 0, (tokens // GROUP) * SLOTS + taken, -1)
+    return send_slot[None, :], source[:, None]
+
+
+def route_kernel(slot_ref, source_ref, merged_ref, cache_ref, packed, landed, total, send_sem, land_sem):
+    n_batch = lax.axis_size("batch")
+    me = lax.axis_index("batch")
+    barrier = pltpu.get_barrier_semaphore()
+
+    @pl.loop(1, n_batch)
+    def _(step):
+        pl.semaphore_signal(barrier, inc=1, device_id={"batch": lax.rem(me + step, n_batch)})
+
+    pl.semaphore_wait(barrier, n_batch - 1)
+
+    def copy(step):
+        return pltpu.make_async_remote_copy(
+            src_ref=packed.at[step],
+            dst_ref=landed.at[step],
+            send_sem=send_sem.at[step],
+            recv_sem=land_sem.at[step],
+            device_id={"batch": lax.rem(me + step, n_batch)},
+        )
+
+    @pl.loop(0, n_batch // PER)
+    def _(part):
+        for inner in range(PER):
+            step = part * PER + inner
+            owner = lax.rem(me + step, n_batch)
+            wanted = lax.broadcasted_iota(jnp.int32, (SLOTS, GROUP), 0) + owner * SLOTS
+            picks = jnp.where(slot_ref[...] == wanted, 1.0, 0.0).astype(jnp.bfloat16)
+            rows = jnp.dot(picks, merged_ref[...], preferred_element_type=jnp.float32)
+            packed[step] = rows.astype(jnp.bfloat16)
+        for inner in range(PER):
+            step = part * PER + inner
+
+            @pl.when(step > 0)
+            def _():
+                copy(step).start()
+
+    landed[0] = packed[0]
+
+    for part in range(n_batch // PER):
+        marks = []
+        blocks = []
+        for inner in range(PER):
+            step = part * PER + inner
+            if step > 0:
+                copy(step).wait_recv()
+            blocks.append(landed[step])
+            group = lax.rem(me - step + n_batch, n_batch)
+            marks.append(lax.broadcasted_iota(jnp.int32, (1, SLOTS), 1) + group * SLOTS)
+        marks = jnp.concatenate(marks, axis=1)
+        blocks = jnp.concatenate(blocks, axis=0)
+
+        @pl.loop(0, ROWS // 256)
+        def _(tile):
+            rows = pl.ds(pl.multiple_of(tile * 256, 256), 256)
+            picks = jnp.where(source_ref[rows, :] == marks, 1.0, 0.0).astype(jnp.bfloat16)
+            placed = jnp.dot(picks, blocks, preferred_element_type=jnp.float32)
+            if part == 0:
+                total[rows, :] = placed
+            else:
+                total[rows, :] += placed
+
+    cache_ref[...] = total[:CAP, :].astype(jnp.bfloat16)
+
+    @pl.loop(1, n_batch)
+    def _(step):
+        copy(step).wait_send()
+
+
+def route(send_slot, source, merged):
+    n_batch = lax.axis_size("batch")
+    features = merged.shape[1]
+    vmem = pl.BlockSpec(memory_space=pltpu.VMEM)
+    return pl.pallas_call(
+        route_kernel,
+        out_shape=jax.ShapeDtypeStruct((CAP, features), jnp.bfloat16),
+        in_specs=[vmem] * 3,
+        out_specs=vmem,
+        scratch_shapes=[
+            pltpu.VMEM((n_batch, SLOTS, features), jnp.bfloat16),
+            pltpu.VMEM((n_batch, SLOTS, features), jnp.bfloat16),
+            pltpu.VMEM((ROWS, features), jnp.float32),
+            pltpu.SemaphoreType.DMA((n_batch,)),
+            pltpu.SemaphoreType.DMA((n_batch,)),
+        ],
+        compiler_params=pltpu.CompilerParams(
+            collective_id=0, has_side_effects=True, vmem_limit_bytes=40 * 1024 * 1024
+        ),
+    )(send_slot, source, merged)
 
 
 def shards(
@@ -111,23 +227,8 @@
     normed = rms_scaled(resid, merge_gain)
     merged = normed.reshape(rows_here // 4, 4 * width).astype(jnp.bfloat16)
     grouped = lax.all_to_all(merged, "seq", split_axis=1, concat_axis=0, tiled=True)
-    group_size = grouped.shape[0]
-    feature_cols = grouped.shape[1]
-    slot_size = 2 * (group_size // REQS) - 1
-    capacity = REQS * slot_size
-    slot_owner, slot_row = slot_tables(token_lists, req_owner, req_counts, slot_size)
-    mine = slot_owner == batch_place
-    sources = (
-        jnp.full((capacity + 1,), -1, jnp.int32)
-        .at[jnp.where(mine, slot_row, capacity)]
-        .set(token_lists)[:capacity]
-    )
-    blank = jnp.zeros((capacity, feature_cols), jnp.bfloat16)
-    group_piece = lax.all_gather(grouped, "batch", axis=0, tiled=True)
-    present = (sources >= 0) & (sources < group_piece.shape[0])
-    chosen = jnp.take(group_piece, jnp.clip(sources, 0, group_piece.shape[0] - 1), axis=0)
-    cache_rows = jnp.where(present[:, None], chosen, blank)
-    return cache_rows[None]
+    send_slot, source = routing_tables(token_lists, req_owner, req_counts, batch_place, batch_place)
+    return route(send_slot, source, grouped)[None]
 
 
 def solution(mesh):

time: 452 us -> 290 us (0.64)
  local copies, waits for them, and re-layouts: 117 us -> 31 us
  waiting for transfers between devices: 182 us -> 101 us
  blocking collectives: 74.6 us -> 6.51 us
  Pallas kernels: 0 us -> 50 us
  other arithmetic: 11.6 us -> 20.5 us
  between operations: 14 us -> 21.8 us
    all_gather x1 -> x0, waiting for transfers between devices: 106 us -> none  [shards(): group_piece = lax.all_gather(grouped, 'batch', axis=0, tiled=True)]
    scatter x1 -> x0, local copies, waits for them, and re-layouts: 75.5 us -> none  [shards(): sources = jnp.full((capacity + 1,), -1, jnp.int32).at[jnp.where(mine, slo...]
    unnamed x1, blocking collectives: 57.6 us -> 6.51 us
    pallas_call x0 -> x1, Pallas kernels: none -> 50 us  [route(): pl.pallas_call(route_kernel, out_shape=jax.ShapeDtypeStruct((CAP, feature...]
    all_to_all x1, waiting for transfers between devices: 0.01 us -> 41 us  [shards(): lax.all_to_all(qkv_own, 'seq', split_axis=2, concat_axis=0, tiled=True)]
    all_gather x1, waiting for transfers between devices: 61.2 us -> 39.2 us  [shards(): lax.all_gather(w_qkv, 'seq', axis=2, tiled=True)]
    all_to_all x1 -> x0, blocking collectives: 17 us -> none  [shards(): lax.all_to_all(merged, 'seq', split_axis=1, concat_axis=0, tiled=True)]
    gather x1 -> x0, local copies, waits for them, and re-layouts: 16.3 us -> none  [shards(): jnp.take(group_piece, jnp.clip(sources, 0, group_piece.shape[0] - 1), axi...]
  transfers between devices with their start and end apart: 5 -> 5, of which waited for: 3 -> 4; matrix products, arithmetic and copies ran while one was open for 27% -> 27% of each run, Pallas kernels for 0% -> 0%
where the time goes in v1:
time: 290 us; the launch traced here: 287 us
  waiting for transfers between devices  101 us (35%)
  Pallas kernels  50 us (17%)
  matrix products  36.7 us (13%)
  local copies, waits for them, and re-layouts  31 us (11%)
  between operations  21.8 us (8%)
  other arithmetic  20.5 us (7%)
  starting transfers between devices  16.1 us (6%)
  blocking collectives  6.51 us (2%)
  loops' own time  3.58 us (1%)
    pallas_call x1, Pallas kernels, route(): pl.pallas_call(route_kernel, out_shape=jax.ShapeDtypeStruct((CAP, feature...  50 us
    all_to_all x1, waiting for transfers between devices, shards(): lax.all_to_all(qkv_own, 'seq', split_axis=2, concat_axis=0, tiled=True)  41 us
    all_gather x1, waiting for transfers between devices, shards(): lax.all_gather(w_qkv, 'seq', axis=2, tiled=True)  39.2 us
    dot_general x5, matrix products, one_block(): jnp.einsum('hqk,khd->qhd', weights, value_block, preferred_element_type=j...  15.9 us
    dot_general x1, matrix products, shards(): jnp.einsum('rw,iwc->ric', normalized, lax.all_gather(w_qkv, 'seq', axis=2...  10.6 us
    all_to_all x1, waiting for transfers between devices, shards(): lax.all_to_all(attended_local, 'seq', split_axis=0, concat_axis=1, tiled=...  10.4 us
    all_to_all x1, waiting for transfers between devices, shards(): lax.all_to_all(merged, 'seq', split_axis=1, concat_axis=0, tiled=True)  9.02 us
    all_to_all x3, local copies, waits for them, and re-layouts, shards(): lax.all_to_all(qkv_own, 'seq', split_axis=2, concat_axis=0, tiled=True)  7.14 us
  transfers between devices with their start and end apart: 5, of which 4 were waited for; matrix products, arithmetic and copies ran while one was open for 27% of the time, Pallas kernels for 0%

profile of v1, /device:TPU:27, one launch (start us, length us, event | category | flops | bytes accessed | tf_op | source)
XLA Modules:
  0.0 287.2 jit_solution(16819798376469111489)
XLA Ops:
  6.6 0.7 all-gather.3.cloned.1.call-update
  7.3 0.7 all-gather.5.cloned.1.call-update
  8.0 0.7 broadcast_compare_fusion.2
  8.8 0.8 copy.57
  9.8 1.5 select_reduce_fusion.3
  18.8 3.4 %fusion.61 = (s32[319]{0:T(512)S(1)}, s32[319]{0:T(512)S(1)}, s32[319]{0:T(512)S(1)}, s32[319]{0:T(512)S(1)}) fusion(s32[]{:T(128)S(6)} %select_n.117, s32[20480]{0:T(1024)} %param.21, s32[]{:T(128)} %get-tuple-element.48, s32[]{:T(128)S(6)} %select_n.109, s32[]{:T(128)} %get-tuple-element.49, s32[]{:T(128)S(6)} %select_n.113, s32[]{:T(128)} %get-tuple-element.51, ...), kind=kLoop, calls=%fused_computation.76 | loop fusion | flops 2552 | bytes 87056 | tf_op jit(solution)/shard_map/jit(_where)/select_n | solution.py:88
  23.8 6.5 %all-reduce.4 = s32[640]{0:T(1024)S(1)} all-reduce(s32[640]{0:T(1024)S(1)} %bitcast_dynamic-update-slice_fusion), channel_id=1, replica_groups=mesh['seq'=8,'batch'=32] {'seq'}, use_global_device_ids=true, to_apply=%add.4 | all-reduce | flops 640 | bytes 5120
  30.9 39.2 %all-gather.3.cloned.1.call-done = bf16[3,1280,1280]{1,2,0:T(8,128)(2,1)} async-done(((bf16[3,1280,160]{1,2,0:T(8,128)(2,1)}), bf16[3,1280,1280]{1,2,0:T(8,128)(2,1)}) %all-gather.3.cloned.1.call-update) | async-done | bytes 9830416 | tf_op jit(solution)/shard_map/all_gather | solution.py:214
  70.0 10.6 %add_convert_fusion = bf16[320,3,1280]{2,0,1:T(8,128)(2,1)S(1)} fusion(bf16[3,1280,1280]{1,2,0:T(8,128)(2,1)} %all-gather.3.cloned.1.call-done, f32[3,1280]{1,0:T(4,128)S(1)} %copy-done.6, bf16[1,320,1280]{2,1,0:T(8,128)(2,1)S(1)} %copy-done.1, f32[1280]{0:T(1024)S(1)} %copy-done.7, f32[320]{0:T(512)S(1)} %add_rsqrt_fusion.1), kind=kOutput, calls=%fused_computation.34 | convolution fusion | flops 3149824000 | bytes 13128960 | tf_op jit(solution)/shard_map/rw,iwc->ric/dot_general | solution.py:211
  80.6 6.2 %copy.67 = bf16[320,3,1280]{0,1,2:T(4,128)(2,1)} copy(bf16[320,3,1280]{2,0,1:T(8,128)(2,1)S(1)} %add_convert_fusion) | data formatting | bytes 4915200 | tf_op jit(solution)/shard_map/convert_element_type | solution.py:217
  86.9 5.7 %all-to-all-start = ((bf16[320,3,1280]{0,1,2:T(4,128)(2,1)}), bf16[320,3,1280]{0,1,2:T(4,128)(2,1)}, u32[]{:S(2)}, u32[]{:S(2)}) async-start(bf16[320,3,1280]{0,1,2:T(4,128)(2,1)} %copy.67), calls=%async_computation | async-start | bytes 7864320 | tf_op jit(solution)/shard_map/all_to_all | solution.py:218
  92.6 3.0 %select_reduce_fusion.1 = s32[20480]{0:T(1024)S(1)} fusion(s32[128]{0:T(128)S(1)} %copy-done.5, s32[128]{0:T(128)S(1)} %reduce, s32[128]{0:T(128)S(1)} %get-tuple-element.78), kind=kLoop, calls=%fused_computation.29 | loop fusion | flops 13086720 | bytes 83456 | tf_op jit(solution)/shard_map/reduce_sum | solution.py:71
  95.6 7.1 %select_reduce_fusion = s32[640]{0:T(1024)S(1)} fusion(s32[20480]{0:T(1024)S(1)} %select_reduce_fusion.1, s32[640]{0:T(1024)S(1)} %iota_add_fusion, s32[20480]{0:T(1024)S(1)} %copy-done.3), kind=kLoop, calls=%fused_computation.28 | loop fusion | flops 39320960 | bytes 168960 | tf_op jit(solution)/shard_map/reduce_sum | solution.py:73
  102.7 41.0 %all-to-all-done = bf16[320,3,1280]{0,1,2:T(4,128)(2,1)} async-done(((bf16[320,3,1280]{0,1,2:T(4,128)(2,1)}), bf16[320,3,1280]{0,1,2:T(4,128)(2,1)}, u32[]{:S(2)}, u32[]{:S(2)}) %all-to-all-start) | async-done | bytes 2457632 | tf_op jit(solution)/shard_map/all_to_all | solution.py:218
  143.7 2.5 copy.68
  146.2 1.1 copy.69
  147.4 3.5 %all_to_all.42 = bf16[2560,3,160]{0,2,1:T(8,128)(2,1)} reshape(bf16[8,320,3,160]{1,0,3,2:T(8,128)(2,1)S(1)} %copy.69) | data formatting | bytes 4915200 | tf_op jit(solution)/shard_map/all_to_all | solution.py:218
  150.8 1.8 fusion.67
  153.3 31.6 %while.10 = (s32[]{:T(128)}, bf16[5,512,2,80]{1,3,2,0:T(8,128)(2,1)}, s32[5]{0:T(128)S(1)}, bf16[2686,2,80]{0,2,1:T(8,128)(2,1)S(1)}, s32[2560]{0:T(1024)S(1)}, ...) while((s32[]{:T(128)}, ...), condition=%wide.region_18.19_spmd, body=%wide.region_15.18_spmd.sunk | while | flops 319880448 | bytes 2112200 | solution.py:52
  153.3 0.7 dynamic_slice.86
  155.1 1.4 fusion.83
  156.5 3.2 %fusion.84 = bf16[5,512,2,80]{1,3,2,0:T(8,128)(2,1)} fusion(bf16[5,512,2,80]{1,3,2,0:T(8,128)(2,1)} %get-tuple-element.151, s32[]{:T(128)} %get-tuple-element.150, f32[2,512]{1,0:T(2,128)S(1)} %fusion.83, bf16[2686,2,80]{0,2,1:T(8,128)(2,1)S(1)} %get-tuple-element.166, s32[]{:T(128)S(6)} %select_n.157, ...), kind=kOutput, calls=%fused_computation.11.clone.1 | convolution fusion | flops 212409984 | bytes 1071104 | tf_op jit(solution)/shard_map/while/body/eval_jaxpr/hqk,khd->qhd/dot_general | solution.py:49
  159.7 0.7 dynamic_slice.86
  161.4 1.4 fusion.83
  162.8 3.2 %fusion.84 = bf16[5,512,2,80]{1,3,2,0:T(8,128)(2,1)} fusion(bf16[5,512,2,80]{1,3,2,0:T(8,128)(2,1)} %get-tuple-element.151, s32[]{:T(128)} %get-tuple-element.150, f32[2,512]{1,0:T(2,128)S(1)} %fusion.83, bf16[2686,2,80]{0,2,1:T(8,128)(2,1)S(1)} %get-tuple-element.166, s32[]{:T(128)S(6)} %select_n.157, ...), kind=kOutput, calls=%fused_computation.11.clone.1 | convolution fusion | flops 212409984 | bytes 1071104 | tf_op jit(solution)/shard_map/while/body/eval_jaxpr/hqk,khd->qhd/dot_general | solution.py:49
  166.0 0.7 dynamic_slice.86
  167.8 1.4 fusion.83
  169.1 3.2 %fusion.84 = bf16[5,512,2,80]{1,3,2,0:T(8,128)(2,1)} fusion(bf16[5,512,2,80]{1,3,2,0:T(8,128)(2,1)} %get-tuple-element.151, s32[]{:T(128)} %get-tuple-element.150, f32[2,512]{1,0:T(2,128)S(1)} %fusion.83, bf16[2686,2,80]{0,2,1:T(8,128)(2,1)S(1)} %get-tuple-element.166, s32[]{:T(128)S(6)} %select_n.157, ...), kind=kOutput, calls=%fused_computation.11.clone.1 | convolution fusion | flops 212409984 | bytes 1071104 | tf_op jit(solution)/shard_map/while/body/eval_jaxpr/hqk,khd->qhd/dot_general | solution.py:49
  172.3 0.7 dynamic_slice.86
  174.1 1.4 fusion.83
  175.4 3.2 %fusion.84 = bf16[5,512,2,80]{1,3,2,0:T(8,128)(2,1)} fusion(bf16[5,512,2,80]{1,3,2,0:T(8,128)(2,1)} %get-tuple-element.151, s32[]{:T(128)} %get-tuple-element.150, f32[2,512]{1,0:T(2,128)S(1)} %fusion.83, bf16[2686,2,80]{0,2,1:T(8,128)(2,1)S(1)} %get-tuple-element.166, s32[]{:T(128)S(6)} %select_n.157, ...), kind=kOutput, calls=%fused_computation.11.clone.1 | convolution fusion | flops 212409984 | bytes 1071104 | tf_op jit(solution)/shard_map/while/body/eval_jaxpr/hqk,khd->qhd/dot_general | solution.py:49
  180.4 1.4 fusion.83
  181.7 3.2 %fusion.84 = bf16[5,512,2,80]{1,3,2,0:T(8,128)(2,1)} fusion(bf16[5,512,2,80]{1,3,2,0:T(8,128)(2,1)} %get-tuple-element.151, s32[]{:T(128)} %get-tuple-element.150, f32[2,512]{1,0:T(2,128)S(1)} %fusion.83, bf16[2686,2,80]{0,2,1:T(8,128)(2,1)S(1)} %get-tuple-element.166, s32[]{:T(128)S(6)} %select_n.157, ...), kind=kOutput, calls=%fused_computation.11.clone.1 | convolution fusion | flops 212409984 | bytes 1071104 | tf_op jit(solution)/shard_map/while/body/eval_jaxpr/hqk,khd->qhd/dot_general | solution.py:49
  184.9 1.6 copy.70
  186.6 1.3 all_to_all.43
  187.9 1.1 copy.71
  189.0 4.9 %all-to-all-start.1 = ((bf16[8,320,160]{1,2,0:T(8,128)(2,1)}), bf16[8,320,160]{1,2,0:T(8,128)(2,1)S(1)}, u32[]{:S(2)}, u32[]{:S(2)}) async-start(bf16[8,320,160]{1,2,0:T(8,128)(2,1)} %copy.71), calls=%async_computation.1 | async-start | bytes 1966080 | tf_op jit(solution)/shard_map/all_to_all | solution.py:220
  194.4 1.1 copy.64
  195.6 0.9 copy.66
  196.9 10.4 %all-to-all-done.1 = bf16[8,320,160]{1,2,0:T(8,128)(2,1)S(1)} async-done(((bf16[8,320,160]{1,2,0:T(8,128)(2,1)}), bf16[8,320,160]{1,2,0:T(8,128)(2,1)S(1)}, u32[]{:S(2)}, u32[]{:S(2)}) %all-to-all-start.1) | async-done | bytes 819232 | tf_op jit(solution)/shard_map/all_to_all | solution.py:220
  207.2 3.4 %multiply_reduce_fusion = (f32[320]{0:T(512)S(1)}, f32[320,1280]{1,0:T(8,128)S(1)}) fusion(f32[1280]{0:T(1024)S(1)} %copy-done.8, bf16[320,1280]{0,1:T(8,128)(2,1)S(1)} %bitcast.53, bf16[1280,1280]{1,0:T(8,128)(2,1)} %all-gather.5.cloned.1.call-done, bf16[1,320,1280]{2,1,0:T(8,128)(2,1)S(1)} %copy-done.2), kind=kOutput, calls=%fused_computation.43 | convolution fusion | flops 1050623680 | bytes 6560000 | tf_op jit(solution)/shard_map/dot_general | solution.py:221
  211.2 1.0 copy.72
  212.1 5.4 %all-to-all-start.2 = ((bf16[80,8,640]{2,0,1:T(8,128)(2,1)}), bf16[80,8,640]{2,0,1:T(8,128)(2,1)S(1)}, u32[]{:S(2)}, u32[]{:S(2)}) async-start(bf16[80,8,640]{2,0,1:T(8,128)(2,1)} %copy.72), calls=%async_computation.2 | async-start | bytes 1638400 | tf_op jit(solution)/shard_map/all_to_all | solution.py:229
  217.6 1.1 convert_reduce_fusion
  218.7 1.4 fusion.53.source_ref
  220.1 9.0 %all-to-all-done.2 = bf16[80,8,640]{2,0,1:T(8,128)(2,1)S(1)} async-done(((bf16[80,8,640]{2,0,1:T(8,128)(2,1)}), bf16[80,8,640]{2,0,1:T(8,128)(2,1)S(1)}, u32[]{:S(2)}, u32[]{:S(2)}) %all-to-all-start.2) | async-done | bytes 819232 | tf_op jit(solution)/shard_map/all_to_all | solution.py:229
  229.1 50.0 %shard_map.109 = bf16[1276,640]{1,0:T(8,128)(2,1)S(1)} custom-call(s32[1,640]{1,0:T(1,128)S(1)} %add.116.slot_ref, s32[1280,1]{1,0:T(8,128)S(1)} %fusion.53.source_ref, bf16[640,640]{1,0:T(8,128)(2,1)S(1)} %bitcast.49), custom_call_target="tpu_custom_call" | custom-call | tf_op jit(solution)/shard_map/pallas_call | solution.py:170
  279.2 1.2 copy.104
  (76 shorter events, 6.7 us)
Async XLA Ops:
  6.5 16.0 %copy-start.10 = (u32[256]{0:T(256)S(1)}, u32[256]{0:T(256)}, u32[]{:S(2)}) copy-start(u32[256]{0:T(256)} %constant.83) | copy-start | bytes 3076
  6.5 15.7 %copy-start.1 = (bf16[1,320,1280]{2,1,0:T(8,128)(2,1)S(1)}, bf16[1,320,1280]{2,1,0:T(8,128)(2,1)}, u32[]{:S(2)}) copy-start(bf16[1,320,1280]{2,1,0:T(8,128)(2,1)} %param.13) | copy-start | bytes 2457604
  6.5 17.2 %copy-start.9 = (s32[1,80]{1,0:T(1,128)S(1)}, s32[1,80]{1,0:T(1,128)}, u32[]{:S(2)}) copy-start(s32[1,80]{1,0:T(1,128)} %param.14) | copy-start | bytes 964
  6.5 63.5 %copy-start.7 = (f32[1280]{0:T(1024)S(1)}, f32[1280]{0:T(1024)}, u32[]{:S(2)}) copy-start(f32[1280]{0:T(1024)} %param.15) | copy-start | bytes 15364
  6.5 63.5 %copy-start.6 = (f32[3,1280]{1,0:T(4,128)S(1)}, f32[3,1280]{1,0:T(4,128)}, u32[]{:S(2)}) copy-start(f32[3,1280]{1,0:T(4,128)} %param.17) | copy-start | bytes 46084
  6.5 63.5 %all-gather.3.cloned.1.call-start = ((), (), s32[]{:S(2)}) async-start(), calls=%async_computation.3 | async-start | bytes 11059200 | tf_op jit(solution)/shard_map/all_gather | solution.py:214
  7.3 189.6 %all-gather.5.cloned.1.call-start = ((), (), s32[]{:S(2)}) async-start(), calls=%async_computation.4 | async-start | bytes 3686400 | tf_op jit(solution)/shard_map/all_gather | solution.py:223
  86.9 5.7 %copy-start.5 = (s32[128]{0:T(128)S(1)}, s32[128]{0:T(128)}, u32[]{:S(2)}) copy-start(s32[128]{0:T(128)} %param.22) | copy-start | bytes 1540
  86.9 8.7 %copy-start.3 = (s32[20480]{0:T(1024)S(1)}, s32[20480]{0:T(1024)}, u32[]{:S(2)}) copy-start(s32[20480]{0:T(1024)} %param.21) | copy-start | bytes 245764
  86.9 56.8 %all-to-all-start = ((bf16[320,3,1280]{0,1,2:T(4,128)(2,1)}), bf16[320,3,1280]{0,1,2:T(4,128)(2,1)}, u32[]{:S(2)}, u32[]{:S(2)}) async-start(bf16[320,3,1280]{0,1,2:T(4,128)(2,1)} %copy.67), calls=%async_computation | async-start | bytes 7864320 | tf_op jit(solution)/shard_map/all_to_all | solution.py:218
  187.9 19.3 %copy-start.2 = (bf16[1,320,1280]{2,1,0:T(8,128)(2,1)S(1)}, bf16[1,320,1280]{2,1,0:T(8,128)(2,1)}, u32[]{:S(2)}) copy-start(bf16[1,320,1280]{2,1,0:T(8,128)(2,1)} %param.13) | copy-start | bytes 2457604
  187.9 19.3 %copy-start.8 = (f32[1280]{0:T(1024)S(1)}, f32[1280]{0:T(1024)}, u32[]{:S(2)}) copy-start(f32[1280]{0:T(1024)} %param.19) | copy-start | bytes 15364
  189.0 18.2 %all-to-all-start.1 = ((bf16[8,320,160]{1,2,0:T(8,128)(2,1)}), bf16[8,320,160]{1,2,0:T(8,128)(2,1)S(1)}, u32[]{:S(2)}, u32[]{:S(2)}) async-start(bf16[8,320,160]{1,2,0:T(8,128)(2,1)} %copy.71), calls=%async_computation.1 | async-start | bytes 1966080 | tf_op jit(solution)/shard_map/all_to_all | solution.py:220
  207.2 3.4 %copy-start.4 = (f32[1280]{0:T(1024)S(1)}, f32[1280]{0:T(1024)}, u32[]{:S(2)}) copy-start(f32[1280]{0:T(1024)} %param.20) | copy-start | bytes 15364
  211.1 7.6 %copy-start = (s32[1280,1]{1,0:T(8,128)S(1)}, s32[1280,1]{1,0:T(8,128)}, u32[]{:S(2)}) copy-start(s32[1280,1]{1,0:T(8,128)} %copy.64) | copy-start | bytes 15364
  212.1 17.0 %all-to-all-start.2 = ((bf16[80,8,640]{2,0,1:T(8,128)(2,1)}), bf16[80,8,640]{2,0,1:T(8,128)(2,1)S(1)}, u32[]{:S(2)}, u32[]{:S(2)}) async-start(bf16[80,8,640]{2,0,1:T(8,128)(2,1)} %copy.72), calls=%async_computation.2 | async-start | bytes 1638400 | tf_op jit(solution)/shard_map/all_to_all | solution.py:229
Sparse Core Ops, SparseCore 0:
  9.2 60.7 all-gather.2
  71.9 41.9 all-gather.4

commit v2 on v1

--- a/solution.py
+++ b/solution.py
@@ -7,9 +7,10 @@
 from jax.experimental.pallas import tpu as pltpu
 from jax.sharding import PartitionSpec as P
 
-HEADS = 16
 REQS = 4
-HALO = 63
+WIDTH = 1280
+TALL = 2688
+SCALE = math.log2(math.e) / math.sqrt(80)
 SLOTS = 40
 GROUP = 640
 TOKENS = 20480
@@ -19,48 +20,343 @@
 PER = 8
 
 
-def rms_scaled(values, gain):
-    return values * lax.rsqrt(jnp.mean(values * values, axis=-1, keepdims=True) + 1e-06) * gain
-
-
-def band_attend(queries, keys_band, values_band, query_ids, key_ids, margin):
-    row_count = queries.shape[0]
-    block_rows = min(512, row_count)
-    block_count = row_count // block_rows
-    band_width = block_rows + 2 * margin
-    scaling = 1.0 / math.sqrt(queries.shape[2])
-
-    def one_block(block_index):
-        starting = block_index * block_rows
-        query_block = lax.dynamic_slice_in_dim(queries, starting, block_rows, 0)
-        key_block = lax.dynamic_slice_in_dim(keys_band, starting, band_width, 0)
-        value_block = lax.dynamic_slice_in_dim(values_band, starting, band_width, 0)
-        own_ids = lax.dynamic_slice_in_dim(query_ids, starting, block_rows, 0)
-        other_ids = lax.dynamic_slice_in_dim(key_ids, starting, band_width, 0)
-        matches = own_ids[:, None] == other_ids[None, :]
-        scores = (
-            jnp.einsum("qhd,khd->hqk", query_block, key_block, preferred_element_type=jnp.float32)
-            * scaling
-        )
-        scores = jnp.where(matches[None], scores, -1e30)
-        maxima = jnp.max(scores, axis=2, keepdims=True)
-        exponent = jnp.exp(scores - maxima)
-        weights = (exponent / jnp.sum(exponent, axis=2, keepdims=True)).astype(jnp.bfloat16)
-        mixed = jnp.einsum("hqk,khd->qhd", weights, value_block, preferred_element_type=jnp.float32)
-        return mixed.astype(jnp.bfloat16)
-
-    attended = lax.map(one_block, jnp.arange(block_count, dtype=jnp.int32))
-    return attended.reshape(row_count, -1)
-
-
-def attend_sequence(qkv_rows, head_count, padded_ids, query_ids):
-    row_count = qkv_rows.shape[0]
-    head_size = qkv_rows.shape[2] // head_count
-    widths = ((HALO, HALO), (0, 0), (0, 0))
-    queries = qkv_rows[:, 0].reshape(row_count, head_count, head_size)
-    keys_band = jnp.pad(qkv_rows[:, 1].reshape(row_count, head_count, head_size), widths)
-    values_band = jnp.pad(qkv_rows[:, 2].reshape(row_count, head_count, head_size), widths)
-    return band_attend(queries, keys_band, values_band, query_ids, padded_ids, HALO)
+def dot(left, right, dims=((1,), (0,))):
+    return lax.dot_general(left, right, (dims, ((), ())), preferred_element_type=jnp.float32)
+
+
+def iota(shape, axis):
+    return lax.broadcasted_iota(jnp.int32, shape, axis)
+
+
+def onehot(condition):
+    return jnp.where(condition, 1.0, 0.0).astype(jnp.bfloat16)
+
+
+def encode_kernel(
+    patch_ref, ids_ref, gain_ref, w_ref, b_ref, wproj_ref, bproj_ref, merge_ref, merged_ref,
+    raw, xn, wt, bias, q, kv, perm, id_send, id_land, id_row, id_col, attn, pieces, mixed, wp, resid,
+    sums_out, sums_in, x_send, x_land, d_send, d_land, i_send, i_land, ws_sem, wx_sem, wy_sem,
+    a_send, a_land, f_send, f_land, s_sem,
+):
+    place = lax.axis_index("seq")
+    batch = lax.axis_index("batch")
+    x, core = place // 2, place % 2
+    row_y = batch % 4
+    column = batch - row_y
+    sibling = place + 1 - 2 * core
+    right = lax.rem(x + 1, 4) * 2 + core
+    left = lax.rem(x + 3, 4) * 2 + core
+    barrier = pltpu.get_barrier_semaphore()
+
+    for step in range(1, 8):
+        pl.semaphore_signal(barrier, inc=1, device_id={"seq": lax.rem(place + step, 8)})
+    for step in range(1, 4):
+        pl.semaphore_signal(barrier, inc=1, device_id={"batch": column + lax.rem(row_y + step, 4)})
+    pl.semaphore_wait(barrier, 10)
+
+    def rows_of(chip, half=None):
+        start = lax.rem(chip, 4) * 640 + core * 320
+        if half is None:
+            return pl.ds(pl.multiple_of(start, 32), 320)
+        return pl.ds(pl.multiple_of(start + half * 160, 32), 160)
+
+    def remote(src, dst, send, land, **device):
+        return pltpu.make_async_remote_copy(
+            src_ref=src, dst_ref=dst, send_sem=send, recv_sem=land, device_id=device
+        )
+
+    def ring(which):
+        half = (0, 1, 1, 0, 0, 1)[which]
+        target = (right, left, right, left, right, left)[which]
+        if which < 4:
+            src = patch_ref.at[pl.ds(half * 160, 160), :]
+            dst = raw.at[rows_of(x, half), :]
+        else:
+            rows = rows_of(x + 3 if which == 4 else x + 1, half)
+            src, dst = raw.at[rows, :], raw.at[rows, :]
+        return remote(src, dst, x_send.at[which], x_land.at[which], seq=target)
+
+    def share(which):
+        if which == 6:
+            return remote(patch_ref, raw.at[rows_of(x), :], d_send.at[6], d_land.at[6], seq=sibling)
+        chip = x + (3, 1, 3, 1, 2, 2)[which]
+        rows = rows_of(chip, (0, 1, 1, 0, 0, 1)[which])
+        return remote(raw.at[rows, :], raw.at[rows, :], d_send.at[which], d_land.at[which], seq=sibling)
+
+    def id_copy(step):
+        return remote(
+            id_send, id_land.at[place], i_send.at[step], i_land.at[step], seq=lax.rem(place + step, 8)
+        )
+
+    own_wrows = pl.ds(pl.multiple_of(place * 160, 32), 160)
+
+    def wp_swap():
+        columns = pl.ds(pl.multiple_of((1 - core) * 640, 128), 640)
+        return remote(wproj_ref.at[:, columns], wp.at[own_wrows, :], ws_sem.at[0], ws_sem.at[1], seq=sibling)
+
+    def wp_part(chip):
+        return pl.ds(pl.multiple_of(lax.rem(chip, 4) * 320 + row_y * 80, 16), 80)
+
+    def wp_x(dx):
+        rows = wp_part(x)
+        target = lax.rem(x + dx, 4) * 2 + core
+        return remote(wp.at[rows, :], wp.at[rows, :], wx_sem.at[0, dx - 1], wx_sem.at[1, dx - 1], seq=target)
+
+    def wp_y(dx, dy):
+        rows = wp_part(x + 4 - dx)
+        index = (dx - 1) * 3 + dy - 1
+        return remote(
+            wp.at[rows, :], wp.at[rows, :], wy_sem.at[0, index], wy_sem.at[1, index],
+            batch=column + lax.rem(row_y + dy, 4),
+        )
+
+    id_send[...] = jnp.zeros_like(id_send)
+    id_send[0:1, 0:80] = ids_ref[...]
+    share(6).start()
+    ring(0).start()
+    ring(1).start()
+    for step in range(1, 8):
+        id_copy(step).start()
+    wp_swap().start()
+    ring(2).start()
+    ring(3).start()
+
+    wp[own_wrows, :] = wproj_ref[:, pl.ds(pl.multiple_of(core * 640, 128), 640)]
+    raw[rows_of(x), :] = patch_ref[...]
+    id_land[place] = id_send[...]
+    xn[0:64, :] = jnp.zeros((64, WIDTH), jnp.bfloat16)
+    xn[TALL - 64 : TALL, :] = jnp.zeros((64, WIDTH), jnp.bfloat16)
+    identity = onehot(iota((160, 160), 0) == iota((160, 160), 1))
+    for which in range(3):
+        rows = pl.ds(which * 160, 160)
+        wt[rows, :] = dot(identity, w_ref[which], ((1,), (1,))).astype(jnp.bfloat16)
+        lanes = iota((160, WIDTH), 1) == iota((160, WIDTH), 0) + place * 160
+        picked = jnp.sum(jnp.where(lanes, b_ref[which : which + 1, :], 0.0), axis=1, keepdims=True)
+        bias[rows, :] = jnp.broadcast_to(picked, (160, 128))
+    inner = iota((512, 512), 1)
+    perm[...] = onehot(iota((512, 512), 0) == (inner & 127) * 4 + (inner >> 7))
+
+    def project(first, count, xrow, columns, out, out_row, wide):
+        del wide
+        product = dot(wt[first : first + count, :], xn[xrow, :], ((1,), (1,)))
+        product = product + bias[first : first + count, 0:1]
+        out[out_row : out_row + count, columns] = product.astype(jnp.bfloat16)
+
+    def attend(block):
+        own = pl.ds(pl.multiple_of(block * 128, 128), 128)
+        band = pl.ds(pl.multiple_of(block * 128, 128), 256)
+        matches = id_col[band, :] == id_row[0:1, own]
+        for head in range(2):
+            feats = pl.ds(head * 80, 80)
+            scores = dot(kv[feats, band], q[feats, own], ((0,), (0,)))
+            scores = jnp.where(matches, scores, -1e30)
+            peak = jnp.max(scores, axis=0, keepdims=True)
+            weights = jnp.exp2((scores - peak) * SCALE)
+            total = jnp.sum(weights, axis=0, keepdims=True)
+            out = dot(kv[pl.ds(160 + head * 80, 80), band], weights.astype(jnp.bfloat16))
+            attn[feats, own] = (out * (1.0 / total)).astype(jnp.bfloat16)
+
+    def take_chip(chip):
+        chip = lax.rem(chip, 4)
+        base = chip * 640
+
+        @pl.loop(0, 10)
+        def _(tile):
+            start = pl.multiple_of(base + tile * 64, 64)
+            rows = raw[pl.ds(start, 64), :].astype(jnp.float32)
+            level = lax.rsqrt(jnp.mean(rows * rows, axis=1, keepdims=True) + 1e-06)
+            xn[pl.ds(pl.multiple_of(start + 64, 64), 64), :] = (rows * level * gain_ref[...]).astype(jnp.bfloat16)
+
+        project(
+            0, 160, pl.ds(pl.multiple_of(base + 64, 64), 640), pl.ds(pl.multiple_of(base, 128), 640), q, 0, 640
+        )
+        wide = pl.ds(pl.multiple_of(base + 128, 128), 512)
+        project(160, 320, wide, wide, kv, 0, 512)
+
+        units = jnp.concatenate([id_land[chip * 2, 0:1, :], id_land[chip * 2 + 1, 0:1, :]], axis=1)
+        units = units.astype(jnp.float32).astype(jnp.bfloat16)
+        spread = iota((640, 256), 0)
+        spread = onehot(jnp.where(spread < 320, spread >> 2, ((spread - 320) >> 2) + 128) == iota((640, 256), 1))
+        id_row[:, pl.ds(pl.multiple_of(base, 128), 640)] = dot(
+            jnp.broadcast_to(units, (8, 256)), spread, ((1,), (1,))
+        )
+        id_col[pl.ds(pl.multiple_of(base + 64, 64), 640), :] = dot(
+            spread, jnp.broadcast_to(units, (128, 256)), ((1,), (1,))
+        )
+
+        @pl.loop(1, 4)
+        def _(tile):
+            attend(chip * 5 + tile)
+
+    id_col[0:64, :] = jnp.full((64, 128), -1.0, jnp.float32)
+    id_col[TALL - 64 : TALL, :] = jnp.full((64, 128), -1.0, jnp.float32)
+    for step in range(1, 8):
+        id_copy(step).wait_recv()
+    share(6).wait_recv()
+    wp_swap().wait_recv()
+    for dx in range(1, 4):
+        wp_x(dx).start()
+    take_chip(x)
+    for which in (0, 1):
+        ring(which).wait_recv()
+        ring(which + 4).start()
+        share(which).start()
+    for dx in range(1, 4):
+        wp_x(dx).wait_recv()
+        for dy in range(1, 4):
+            wp_y(dx, dy).start()
+    for which in (2, 3):
+        ring(which).wait_recv()
+        share(which).start()
+    share(0).wait_recv()
+    share(2).wait_recv()
+    take_chip(x + 3)
+    share(1).wait_recv()
+    share(3).wait_recv()
+    take_chip(x + 1)
+    for which in (4, 5):
+        ring(which).wait_recv()
+        share(which).start()
+    for which in (4, 5):
+        share(which).wait_recv()
+    take_chip(x + 2)
+
+    @pl.loop(0, 5)
+    def _(edge):
+        columns = pl.ds(pl.multiple_of(edge * 640, 128), 128)
+        project(160, 320, columns, columns, kv, 0, 128)
+
+    @pl.loop(0, 4)
+    def _(chip):
+        attend(chip * 5)
+        attend(chip * 5 + 4)
+
+    def chunk_of(part):
+        return pl.ds(pl.multiple_of(part * 128, 128), 128)
+
+    def feats_of(chip, at):
+        return pl.ds(pl.multiple_of(lax.rem(chip, 4) * 320 + at * 160, 32), 160)
+
+    def a_copy(dx, part):
+        chip = lax.rem(x + dx, 4)
+        return remote(
+            pieces.at[chip, :, chunk_of(part)],
+            mixed.at[feats_of(x, core), chunk_of(part)],
+            a_send.at[dx - 1, part],
+            a_land.at[dx - 1, part],
+            seq=chip * 2 + core,
+        )
+
+    def a_share(dx, part):
+        block = mixed.at[feats_of(x + 4 - dx, core), chunk_of(part)]
+        return remote(block, block, f_send.at[dx, part], f_land.at[dx, part], seq=sibling)
+
+    @pl.loop(0, 5)
+    def _(part):
+        chunk = attn[:, pl.ds(pl.multiple_of(part * 512, 128), 512)]
+        sorted_rows = dot(chunk, perm[...]).astype(jnp.bfloat16)
+        for k in range(4):
+            pieces[k, :, chunk_of(part)] = sorted_rows[:, k * 128 : k * 128 + 128]
+        for dx in (2, 1, 3):
+            a_copy(dx, part).start()
+        mixed[feats_of(x, core), chunk_of(part)] = pieces[x, :, chunk_of(part)]
+        a_share(0, part).start()
+
+    half = pl.ds(pl.multiple_of(core * 640, 128), 640)
+    pick = onehot(iota((128, 512), 1) == iota((128, 512), 0) * 4 + x)
+
+    @pl.loop(0, 5)
+    def _(part):
+        rows = raw[pl.ds(pl.multiple_of(part * 512, 128), 512), half]
+        resid[chunk_of(part), :] = dot(pick, rows) + bproj_ref[:, half]
+
+    for dx in range(1, 4):
+        for dy in range(1, 4):
+            wp_y(dx, dy).wait_recv()
+
+    def s_copy(part):
+        return remote(
+            sums_out.at[chunk_of(part), :], sums_in.at[chunk_of(part), :], s_sem.at[0, part], s_sem.at[1, part],
+            seq=sibling,
+        )
+
+    @pl.loop(0, 5)
+    def _(part):
+        for dx in (1, 3, 2):
+            a_copy(dx, part).wait_recv()
+            a_share(dx, part).start()
+        for dx in (0, 1, 3, 2):
+            a_share(dx, part).wait_recv()
+        rows = resid[chunk_of(part), :] + dot(mixed[:, chunk_of(part)], wp[...], ((0,), (0,)))
+        resid[chunk_of(part), :] = rows
+        total = jnp.sum(rows * rows, axis=1, keepdims=True)
+        sums_out[chunk_of(part), :] = jnp.broadcast_to(total, (128, 128))
+        s_copy(part).start()
+
+    @pl.loop(0, 5)
+    def _(part):
+        s_copy(part).wait_recv()
+        total = sums_out[chunk_of(part), 0:1] + sums_in[chunk_of(part), 0:1]
+        level = lax.rsqrt(total * (1.0 / WIDTH) + 1e-06)
+        merged_ref[chunk_of(part), :] = (resid[chunk_of(part), :] * level * merge_ref[:, half]).astype(jnp.bfloat16)
+
+    for which in range(6):
+        ring(which).wait_send()
+    for which in range(7):
+        share(which).wait_send()
+    for step in range(1, 8):
+        id_copy(step).wait_send()
+    wp_swap().wait_send()
+    for dx in range(1, 4):
+        wp_x(dx).wait_send()
+        for dy in range(1, 4):
+            wp_y(dx, dy).wait_send()
+
+    @pl.loop(0, 5)
+    def _(part):
+        for dx in range(1, 4):
+            a_copy(dx, part).wait_send()
+        for dx in range(4):
+            a_share(dx, part).wait_send()
+        s_copy(part).wait_send()
+
+
+def encode(patches, ids, norm_gain, w_qkv, b_qkv, w_proj, b_proj, merge_gain):
+    vmem = pl.BlockSpec(memory_space=pltpu.VMEM)
+    dma = pltpu.SemaphoreType.DMA
+    bf16, f32 = jnp.bfloat16, jnp.float32
+    return pl.pallas_call(
+        encode_kernel,
+        out_shape=jax.ShapeDtypeStruct((GROUP, GROUP), bf16),
+        in_specs=[vmem] * 8,
+        out_specs=vmem,
+        scratch_shapes=[
+            pltpu.VMEM((2560, WIDTH), bf16),
+            pltpu.VMEM((TALL, WIDTH), bf16),
+            pltpu.VMEM((480, WIDTH), bf16),
+            pltpu.VMEM((480, 128), f32),
+            pltpu.VMEM((160, 2560), bf16),
+            pltpu.VMEM((320, TALL), bf16),
+            pltpu.VMEM((512, 512), bf16),
+            pltpu.VMEM((8, 128), jnp.int32),
+            pltpu.VMEM((8, 8, 128), jnp.int32),
+            pltpu.VMEM((8, 2560), f32),
+            pltpu.VMEM((TALL, 128), f32),
+            pltpu.VMEM((160, 2560), bf16),
+            pltpu.VMEM((4, 160, GROUP), bf16),
+            pltpu.VMEM((WIDTH, GROUP), bf16),
+            pltpu.VMEM((WIDTH, GROUP), bf16),
+            pltpu.VMEM((GROUP, GROUP), f32),
+            pltpu.VMEM((GROUP, 128), f32),
+            pltpu.VMEM((GROUP, 128), f32),
+            dma((6,)), dma((6,)), dma((7,)), dma((7,)), dma((8,)), dma((8,)),
+            dma((2,)), dma((2, 3)), dma((2, 9)),
+            dma((3, 5)), dma((3, 5)), dma((4, 5)), dma((4, 5)), dma((2, 5)),
+        ],
+        compiler_params=pltpu.CompilerParams(
+            collective_id=1, has_side_effects=True, vmem_limit_bytes=56 * 1024 * 1024
+        ),
+    )(patches, ids, norm_gain, w_qkv, b_qkv, w_proj, b_proj, merge_gain)
 
 
 def routing_tables(token_lists, req_owner, req_counts, group, owner):
@@ -186,49 +482,14 @@
 
 
 def shards(
-    patches,
-    window_ids,
-    norm_gain,
-    w_qkv,
-    b_qkv,
-    w_proj,
-    b_proj,
-    merge_gain,
-    token_lists,
-    req_owner,
-    req_counts,
+    patches, window_ids, norm_gain, w_qkv, b_qkv, w_proj, b_proj, merge_gain, token_lists, req_owner, req_counts
 ):
-    seq_count = lax.axis_size("seq")
     batch_place = lax.axis_index("batch")
-    patch_rows = patches[0]
-    rows_here = patch_rows.shape[0]
-    width = patch_rows.shape[1]
-    rows_float = patch_rows.astype(jnp.float32)
-    normalized = rms_scaled(rows_float, norm_gain).astype(jnp.bfloat16)
-    unit_ids = lax.all_gather(window_ids, "seq", axis=1, tiled=True)[0]
-    group_ids = jnp.repeat(unit_ids, 4)
-    padded_ids = jnp.pad(group_ids, (HALO, HALO), constant_values=-1)
-    product = jnp.einsum(
-        "rw,iwc->ric",
-        normalized,
-        lax.all_gather(w_qkv, "seq", axis=2, tiled=True),
-        preferred_element_type=jnp.float32,
+    merged = encode(
+        patches[0], window_ids, norm_gain[None], w_qkv, b_qkv, w_proj, b_proj[None], merge_gain[None]
     )
-    qkv_own = (product + b_qkv[None]).astype(jnp.bfloat16)
-    qkv_group = lax.all_to_all(qkv_own, "seq", split_axis=2, concat_axis=0, tiled=True)
-    attended_local = attend_sequence(qkv_group, HEADS // seq_count, padded_ids, group_ids)
-    attended_own = lax.all_to_all(attended_local, "seq", split_axis=0, concat_axis=1, tiled=True)
-    projected = jnp.dot(
-        attended_own,
-        lax.all_gather(w_proj, "seq", axis=0, tiled=True),
-        preferred_element_type=jnp.float32,
-    )
-    resid = rows_float + projected + b_proj
-    normed = rms_scaled(resid, merge_gain)
-    merged = normed.reshape(rows_here // 4, 4 * width).astype(jnp.bfloat16)
-    grouped = lax.all_to_all(merged, "seq", split_axis=1, concat_axis=0, tiled=True)
     send_slot, source = routing_tables(token_lists, req_owner, req_counts, batch_place, batch_place)
-    return route(send_slot, source, grouped)[None]
+    return route(send_slot, source, merged)[None]
 
 
 def solution(mesh):

time: 290 us -> 163 us (0.56)
  waiting for transfers between devices: 101 us -> 0 us
  Pallas kernels: 50 us -> 122 us
  matrix products: 36.7 us -> 0 us
  local copies, waits for them, and re-layouts: 31 us -> 11.9 us
  starting transfers between devices: 16.1 us -> 0 us
  between operations: 21.8 us -> 7.59 us
  blocking collectives: 6.51 us -> 0 us
  loops' own time: 3.58 us -> 0 us
    pallas_call x0 -> x1, Pallas kernels: none -> 69.8 us  [encode(): pl.pallas_call(encode_kernel, out_shape=jax.ShapeDtypeStruct((GROUP, GROU...]
    all_to_all x3 -> x0, waiting for transfers between devices: 60.3 us -> none  [the longest x1 41 us: shards(): lax.all_to_all(qkv_own, 'seq', split_axis=2, concat_axis=0, tiled=True)]
    all_gather x2 -> x0, waiting for transfers between devices: 39.2 us -> none  [the longest x1 39.2 us: shards(): lax.all_gather(w_qkv, 'seq', axis=2, tiled=True)]
    dot_general x7 -> x0, matrix products: 29.9 us -> none  [the longest x5 15.9 us: one_block(): jnp.einsum('hqk,khd->qhd', weights, value_block, preferred_element_type=j...]
    all_to_all x3 -> x0, starting transfers between devices: 16 us -> none  [the longest x1 5.69 us: shards(): lax.all_to_all(qkv_own, 'seq', split_axis=2, concat_axis=0, tiled=True)]
    all_to_all x5 -> x0, local copies, waits for them, and re-layouts: 9.53 us -> none  [the longest x3 7.14 us: shards(): lax.all_to_all(qkv_own, 'seq', split_axis=2, concat_axis=0, tiled=True)]
    convert_element_type x3 -> x0, local copies, waits for them, and re-layouts: 7.5 us -> none  [the longest x1 6.24 us: shards(): qkv_own = (product + b_qkv[None]).astype(jnp.bfloat16)]
    sub x5 -> x0, matrix products: 6.82 us -> none  [one_block(): exponent = jnp.exp(scores - maxima)]
  transfers between devices with their start and end apart: 5 -> 0, of which waited for: 4 -> 0; matrix products, arithmetic and copies ran while one was open for 27% -> 0% of each run, Pallas kernels for 0% -> 0%
where the time goes in v2:
time: 163 us; the launch traced here: 161 us
  Pallas kernels  122 us (75%)
  other arithmetic  19.5 us (12%)
  local copies, waits for them, and re-layouts  11.9 us (7%)
  between operations  7.59 us (5%)
    pallas_call x1, Pallas kernels, encode(): pl.pallas_call(encode_kernel, out_shape=jax.ShapeDtypeStruct((GROUP, GROU...  69.8 us
    pallas_call x1, Pallas kernels, route(): pl.pallas_call(route_kernel, out_shape=jax.ShapeDtypeStruct((CAP, feature...  52.4 us
    reduce_sum x1, other arithmetic, routing_tables(): jnp.sum(jnp.where(token_lists[:, None] == group * GROUP + local[None, :],...  7.96 us
    unnamed x4, local copies, waits for them, and re-layouts  5.95 us
    reduce_sum x1, other arithmetic, routing_tables(): slot_owner = jnp.sum(jnp.where(inside, req_owner[None, :], 0), axis=1)  3.71 us
    select_n x1, other arithmetic, routing_tables(): held.append(jnp.where(jnp.arange(MOST) < count, listed, -1))  3.35 us

profile of v2, /device:TPU:27, one launch (start us, length us, event | category | flops | bytes accessed | tf_op | source)
XLA Modules:
  0.0 161.2 jit_solution(12119885658575031196)
XLA Ops:
  0.0 0.7 broadcast_compare_fusion.1
  0.7 0.1 convert_reduce_fusion.2
  0.8 1.3 broadcast_in_dim.81.gain_ref
  2.1 1.3 broadcast_in_dim.82.bproj_ref
  3.4 1.3 broadcast_in_dim.83.merge_ref
  4.6 0.8 copy.43
  5.4 0.2 reduce-window.8
  5.6 0.1 reduce
  5.7 1.5 select_reduce_fusion.3
  14.6 3.4 %fusion.10 = (s32[319]{0:T(512)S(1)}, s32[319]{0:T(512)S(1)}, s32[319]{0:T(512)S(1)}, s32[319]{0:T(512)S(1)}) fusion(s32[]{:T(128)S(6)} %select_n.104, s32[20480]{0:T(1024)} %param.19, s32[]{:T(128)} %get-tuple-element.5, s32[]{:T(128)S(6)} %select_n.96, s32[]{:T(128)} %get-tuple-element.6, s32[]{:T(128)S(6)} %select_n.100, s32[]{:T(128)} %get-tuple-element.8, ...), kind=kLoop, calls=%fused_computation.34 | loop fusion | flops 2552 | bytes 87056 | tf_op jit(solution)/shard_map/jit(_where)/select_n | solution.py:384
  18.0 0.1 concatenate.60
  18.1 0.1 concatenate.59
  18.3 1.1 convert_reduce_fusion
  19.4 3.7 %select_reduce_fusion.1 = s32[20480]{0:T(1024)S(1)} fusion(s32[128]{0:T(128)} %param.20, s32[128]{0:T(128)S(1)} %reduce, s32[128]{0:T(128)S(1)} %get-tuple-element.19), kind=kLoop, calls=%fused_computation.1 | loop fusion | flops 13086720 | bytes 83456 | tf_op jit(solution)/shard_map/reduce_sum | solution.py:367
  23.1 8.0 %select_reduce_fusion = s32[640]{0:T(1024)S(1)} fusion(s32[20480]{0:T(1024)S(1)} %select_reduce_fusion.1, s32[640]{0:T(1024)S(1)} %iota_add_fusion, s32[20480]{0:T(1024)} %param.19), kind=kLoop, calls=%fused_computation | loop fusion | flops 39320960 | bytes 168960 | tf_op jit(solution)/shard_map/reduce_sum | solution.py:369
  31.1 0.2 convert_reduce_fusion.1
  31.3 0.3 copy.52
  31.7 0.3 copy.49
  32.0 0.3 copy.44
  32.2 0.3 copy.50
  32.5 0.5 fusion.2.source_ref
  33.0 3.6 %copy.53.w_ref = bf16[3,1280,160]{2,1,0:T(8,128)(2,1)} copy(bf16[3,1280,160]{1,2,0:T(8,128)(2,1)} %param.14) | data formatting | bytes 2457600 | tf_op args[3]
  36.6 69.8 %shard_map.109.merged_ref = bf16[640,640]{1,0:T(8,128)(2,1)} custom-call(bf16[320,1280]{1,0:T(8,128)(2,1)} %bitcast.4, s32[1,80]{1,0:T(1,128)} %ids_ref.1, f32[1,1280]{1,0:T(1,128)} %broadcast_in_dim.81.gain_ref, bf16[3,1280,160]{2,1,0:T(8,128)(2,1)} %copy.53.w_ref, f32[3,1280]{1,0:T(4,128)} %b_ref.1, bf16[160,1280]{1,0:T(8,128)(2,1)} %wproj_ref.1, ...), custom_call_target="tpu_custom_call" | custom-call | tf_op jit(solution)/shard_map/pallas_call | solution.py:328
  106.5 0.0 copy-start
  106.5 1.1 copy-done
  107.6 52.4 %shard_map.110 = bf16[1276,640]{1,0:T(8,128)(2,1)S(1)} custom-call(s32[1,640]{1,0:T(1,128)S(1)} %add.63.slot_ref, s32[1280,1]{1,0:T(8,128)S(1)} %fusion.2.source_ref, bf16[640,640]{1,0:T(8,128)(2,1)S(1)} %copy-done), custom_call_target="tpu_custom_call" | custom-call | tf_op jit(solution)/shard_map/pallas_call | solution.py:466
  160.0 1.2 copy.75
  (12 shorter events, 0.1 us)
Async XLA Ops:
  106.5 1.1 copy-start

commit v3 on v2

--- a/solution.py
+++ b/solution.py
@@ -13,7 +13,6 @@
 SCALE = math.log2(math.e) / math.sqrt(80)
 SLOTS = 40
 GROUP = 640
-TOKENS = 20480
 MOST = 319
 CAP = 1276
 ROWS = 1280
@@ -32,14 +31,105 @@
     return jnp.where(condition, 1.0, 0.0).astype(jnp.bfloat16)
 
 
+def lanes_of(ref, first, count):
+    return jnp.concatenate([ref[pl.ds(first + at, 1), :] for at in range(count)], axis=1)
+
+
+def tables(tok_ref, owner_ref, count_ref, batch, steps, jumps, owners, dests, slot, source):
+    f32 = jnp.float32
+    me = batch.astype(f32)
+    counts = count_ref[...].astype(f32)
+    owner = owner_ref[...].astype(f32)
+
+    def flip(row):
+        return jnp.transpose(jnp.broadcast_to(row, (128, 128)))
+
+    lower = iota((128, 128), 0) < iota((128, 128), 1)
+    owner_down = flip(owner)
+    starts = jnp.sum(jnp.where(lower, flip(counts), 0.0), axis=0, keepdims=True)
+    ranks = jnp.sum(jnp.where(lower & (owner_down == owner), 1.0, 0.0), axis=0, keepdims=True)
+    steps[...] = flip(starts)
+    previous = jnp.where(iota((128, 128), 0) == 0, 0.0, pltpu.roll(owner_down, 1, 0))
+    jumps[...] = owner_down - previous
+    places = (iota((160, 128), 0) * 128 + iota((160, 128), 1)).astype(f32)
+
+    def jump(request, held):
+        return held + jnp.where(places >= steps[pl.ds(request, 1), :], jumps[pl.ds(request, 1), :], 0.0)
+
+    owners[...] = lax.fori_loop(0, 128, jump, jnp.zeros((160, 128), f32), unroll=4)
+    dest = jnp.zeros((160, 128), f32)
+    for rank in range(REQS):
+        chosen = (owner == me) & (ranks == rank)
+        start = jnp.sum(jnp.where(chosen, starts, 0.0), axis=1, keepdims=True)
+        count = jnp.sum(jnp.where(chosen, counts, 0.0), axis=1, keepdims=True)
+        within = (places >= start) & (places < start + count)
+        dest = dest + jnp.where(within, places - start + (MOST * rank + 1), 0.0)
+    dests[...] = dest.astype(jnp.int32) - 1
+
+    def gather(part, sums):
+        rows = pl.ds(pl.multiple_of(part * 8, 8), 8)
+        token = tok_ref[rows, :]
+        local = token - batch * GROUP
+        dest = dests[rows, :]
+        owner = owners[rows, :] + 1.0
+        high = (token >> 7).astype(f32) + 1.0
+        low = (token & 127).astype(f32)
+        down, short = iota((128, 128), 0), iota((16, 128), 0)
+        group_left, group_right, own_left, own_right = [], [], [], []
+        for at in range(8):
+            row = slice(at, at + 1)
+            group_left.append(onehot(down == (local[row] & 127)))
+            group_right.append(jnp.where(short == (local[row] >> 7), owner[row], 0.0).astype(jnp.bfloat16))
+            own_left.append(onehot(down == (dest[row] & 127)))
+            mine = short == (dest[row] >> 7)
+            own_right.append(
+                jnp.concatenate([jnp.where(mine, high[row], 0.0), jnp.where(mine, low[row], 0.0)], axis=0).astype(
+                    jnp.bfloat16
+                )
+            )
+        first = dot(jnp.concatenate(group_left, axis=1), jnp.concatenate(group_right, axis=1), ((1,), (1,)))
+        second = dot(jnp.concatenate(own_left, axis=1), jnp.concatenate(own_right, axis=1), ((1,), (1,)))
+        return sums[0] + first, sums[1] + second
+
+    owner_cols, token_cols = lax.fori_loop(
+        0, 20, gather, (jnp.zeros((128, 16), f32), jnp.zeros((128, 32), f32))
+    )
+    unit = onehot(iota((128, 128), 0) == iota((128, 128), 1))
+    owner_rows = dot(owner_cols.astype(jnp.bfloat16), unit, ((0,), (0,)))
+    token_rows = dot(token_cols.astype(jnp.bfloat16), unit, ((0,), (0,)))
+
+    owner_row = jnp.concatenate([owner_rows[at : at + 1] for at in range(5)], axis=1)
+    before = jnp.zeros((1, GROUP), f32)
+    for at in range(5):
+        same = (owner_cols[:, at : at + 1] == owner_row) & (
+            iota((128, GROUP), 0) + at * 128 < iota((128, GROUP), 1)
+        )
+        before = before + jnp.sum(jnp.where(same, 1.0, 0.0), axis=0, keepdims=True)
+    slot[...] = jnp.broadcast_to((owner_row - 1.0) * SLOTS + before, (8, GROUP))
+
+    token_row = jnp.concatenate(
+        [(token_rows[at : at + 1] - 1.0) * 128 + token_rows[at + 16 : at + 17] for at in range(10)], axis=1
+    )
+    for at in range(10):
+        high = token_cols[:, at : at + 1] - 1.0
+        token = high * 128 + token_cols[:, at + 16 : at + 17]
+        group = jnp.floor((high + 0.5) * 0.2)
+        earlier = jnp.where((token_row < token) & (token_row >= group * GROUP), 1.0, 0.0)
+        taken = jnp.sum(earlier, axis=1, keepdims=True)
+        found = jnp.where(high >= 0.0, group * SLOTS + taken, -1.0)
+        source[at * 128 : at * 128 + 128, :] = jnp.broadcast_to(found, (128, 128))
+
+
 def encode_kernel(
-    patch_ref, ids_ref, gain_ref, w_ref, b_ref, wproj_ref, bproj_ref, merge_ref, merged_ref,
-    raw, xn, wt, bias, q, kv, perm, id_send, id_land, id_row, id_col, attn, pieces, mixed, wp, resid,
+    patch_ref, ids_ref, gain_ref, wt, b_ref, wproj_ref, bproj_ref, merge_ref, tok_ref, owner_ref, count_ref,
+    cache_ref, merged_ref, steps, jumps, owners, dests, slot, source, packed, landed, total_ref, send_sem, land_sem,
+    raw, xn, bias, q, kv, perm, id_send, id_land, id_row, id_col, attn, pieces, mixed, wp, resid,
     sums_out, sums_in, x_send, x_land, d_send, d_land, i_send, i_land, ws_sem, wx_sem, wy_sem,
     a_send, a_land, f_send, f_land, s_sem,
 ):
     place = lax.axis_index("seq")
     batch = lax.axis_index("batch")
+    n_batch = lax.axis_size("batch")
     x, core = place // 2, place % 2
     row_y = batch % 4
     column = batch - row_y
@@ -50,9 +140,12 @@
 
     for step in range(1, 8):
         pl.semaphore_signal(barrier, inc=1, device_id={"seq": lax.rem(place + step, 8)})
-    for step in range(1, 4):
-        pl.semaphore_signal(barrier, inc=1, device_id={"batch": column + lax.rem(row_y + step, 4)})
-    pl.semaphore_wait(barrier, 10)
+
+    @pl.loop(1, n_batch)
+    def _(step):
+        pl.semaphore_signal(barrier, inc=1, device_id={"batch": lax.rem(batch + step, n_batch)})
+
+    pl.semaphore_wait(barrier, 7 + n_batch - 1)
 
     def rows_of(chip, half=None):
         start = lax.rem(chip, 4) * 640 + core * 320
@@ -126,10 +219,8 @@
     id_land[place] = id_send[...]
     xn[0:64, :] = jnp.zeros((64, WIDTH), jnp.bfloat16)
     xn[TALL - 64 : TALL, :] = jnp.zeros((64, WIDTH), jnp.bfloat16)
-    identity = onehot(iota((160, 160), 0) == iota((160, 160), 1))
     for which in range(3):
         rows = pl.ds(which * 160, 160)
-        wt[rows, :] = dot(identity, w_ref[which], ((1,), (1,))).astype(jnp.bfloat16)
         lanes = iota((160, WIDTH), 1) == iota((160, WIDTH), 0) + place * 160
         picked = jnp.sum(jnp.where(lanes, b_ref[which : which + 1, :], 0.0), axis=1, keepdims=True)
         bias[rows, :] = jnp.broadcast_to(picked, (160, 128))
@@ -159,13 +250,14 @@
     def take_chip(chip):
         chip = lax.rem(chip, 4)
         base = chip * 640
+        gain = lanes_of(gain_ref, 0, 10)
 
         @pl.loop(0, 10)
         def _(tile):
             start = pl.multiple_of(base + tile * 64, 64)
             rows = raw[pl.ds(start, 64), :].astype(jnp.float32)
             level = lax.rsqrt(jnp.mean(rows * rows, axis=1, keepdims=True) + 1e-06)
-            xn[pl.ds(pl.multiple_of(start + 64, 64), 64), :] = (rows * level * gain_ref[...]).astype(jnp.bfloat16)
+            xn[pl.ds(pl.multiple_of(start + 64, 64), 64), :] = (rows * level * gain).astype(jnp.bfloat16)
 
         project(
             0, 160, pl.ds(pl.multiple_of(base + 64, 64), 640), pl.ds(pl.multiple_of(base, 128), 640), q, 0, 640
@@ -188,6 +280,7 @@
         def _(tile):
             attend(chip * 5 + tile)
 
+    tables(tok_ref, owner_ref, count_ref, batch, steps, jumps, owners, dests, slot, source)
     id_col[0:64, :] = jnp.full((64, 128), -1.0, jnp.float32)
     id_col[TALL - 64 : TALL, :] = jnp.full((64, 128), -1.0, jnp.float32)
     for step in range(1, 8):
@@ -268,7 +361,7 @@
     @pl.loop(0, 5)
     def _(part):
         rows = raw[pl.ds(pl.multiple_of(part * 512, 128), 512), half]
-        resid[chunk_of(part), :] = dot(pick, rows) + bproj_ref[:, half]
+        resid[chunk_of(part), :] = dot(pick, rows) + lanes_of(bproj_ref, core * 5, 5)
 
     for dx in range(1, 4):
         for dy in range(1, 4):
@@ -298,7 +391,63 @@
         s_copy(part).wait_recv()
         total = sums_out[chunk_of(part), 0:1] + sums_in[chunk_of(part), 0:1]
         level = lax.rsqrt(total * (1.0 / WIDTH) + 1e-06)
-        merged_ref[chunk_of(part), :] = (resid[chunk_of(part), :] * level * merge_ref[:, half]).astype(jnp.bfloat16)
+        merged_ref[chunk_of(part), :] = (resid[chunk_of(part), :] * level * lanes_of(merge_ref, core * 5, 5)).astype(jnp.bfloat16)
+
+    def copy(step):
+        return pltpu.make_async_remote_copy(
+            src_ref=packed.at[step],
+            dst_ref=landed.at[step],
+            send_sem=send_sem.at[step],
+            recv_sem=land_sem.at[step],
+            device_id={"batch": lax.rem(batch + step, n_batch)},
+        )
+
+    @pl.loop(0, n_batch // PER)
+    def _(part):
+        for inner in range(PER):
+            step = part * PER + inner
+            owner = lax.rem(batch + step, n_batch)
+            wanted = (iota((SLOTS, GROUP), 0) + owner * SLOTS).astype(jnp.float32)
+            picks = onehot(slot[0:1, :] == wanted)
+            rows = dot(picks, merged_ref[...])
+            packed[step] = rows.astype(jnp.bfloat16)
+        for inner in range(PER):
+            step = part * PER + inner
+
+            @pl.when(step > 0)
+            def _():
+                copy(step).start()
+
+    landed[0] = packed[0]
+
+    for part in range(n_batch // PER):
+        marks = []
+        blocks = []
+        for inner in range(PER):
+            step = part * PER + inner
+            if step > 0:
+                copy(step).wait_recv()
+            blocks.append(landed[step])
+            group = lax.rem(batch - step + n_batch, n_batch)
+            marks.append((iota((1, SLOTS), 1) + group * SLOTS).astype(jnp.float32))
+        marks = jnp.concatenate(marks, axis=1)
+        blocks = jnp.concatenate(blocks, axis=0)
+
+        @pl.loop(0, ROWS // 256)
+        def _(tile):
+            rows = pl.ds(pl.multiple_of(tile * 256, 256), 256)
+            picks = onehot(source[rows, 0:1] == marks)
+            placed = dot(picks, blocks)
+            if part == 0:
+                total_ref[rows, :] = placed
+            else:
+                total_ref[rows, :] += placed
+
+    cache_ref[...] = total_ref[:CAP, :].astype(jnp.bfloat16)
+
+    @pl.loop(1, n_batch)
+    def _(step):
+        copy(step).wait_send()
 
     for which in range(6):
         ring(which).wait_send()
@@ -321,19 +470,30 @@
         s_copy(part).wait_send()
 
 
-def encode(patches, ids, norm_gain, w_qkv, b_qkv, w_proj, b_proj, merge_gain):
+def encode(*arrays):
     vmem = pl.BlockSpec(memory_space=pltpu.VMEM)
+    n_batch = lax.axis_size("batch")
     dma = pltpu.SemaphoreType.DMA
     bf16, f32 = jnp.bfloat16, jnp.float32
     return pl.pallas_call(
         encode_kernel,
-        out_shape=jax.ShapeDtypeStruct((GROUP, GROUP), bf16),
-        in_specs=[vmem] * 8,
+        out_shape=jax.ShapeDtypeStruct((CAP, GROUP), bf16),
+        in_specs=[vmem] * len(arrays),
         out_specs=vmem,
         scratch_shapes=[
+            pltpu.VMEM((GROUP, GROUP), bf16),
+            pltpu.VMEM((128, 128), f32),
+            pltpu.VMEM((128, 128), f32),
+            pltpu.VMEM((160, 128), f32),
+            pltpu.VMEM((160, 128), jnp.int32),
+            pltpu.VMEM((8, GROUP), f32),
+            pltpu.VMEM((ROWS, 128), f32),
+            pltpu.VMEM((n_batch, SLOTS, GROUP), bf16),
+            pltpu.VMEM((n_batch, SLOTS, GROUP), bf16),
+            pltpu.VMEM((ROWS, GROUP), f32),
+            dma((n_batch,)), dma((n_batch,)),
             pltpu.VMEM((2560, WIDTH), bf16),
             pltpu.VMEM((TALL, WIDTH), bf16),
-            pltpu.VMEM((480, WIDTH), bf16),
             pltpu.VMEM((480, 128), f32),
             pltpu.VMEM((160, 2560), bf16),
             pltpu.VMEM((320, TALL), bf16),
@@ -354,142 +514,27 @@
             dma((3, 5)), dma((3, 5)), dma((4, 5)), dma((4, 5)), dma((2, 5)),
         ],
         compiler_params=pltpu.CompilerParams(
-            collective_id=1, has_side_effects=True, vmem_limit_bytes=56 * 1024 * 1024
+            collective_id=0, has_side_effects=True, vmem_limit_bytes=56 * 1024 * 1024
         ),
-    )(patches, ids, norm_gain, w_qkv, b_qkv, w_proj, b_proj, merge_gain)
-
-
-def routing_tables(token_lists, req_owner, req_counts, group, owner):
-    ends = jnp.cumsum(req_counts)
-    starts = ends - req_counts
-    slots = jnp.arange(TOKENS, dtype=jnp.int32)
-    inside = (slots[:, None] >= starts[None, :]) & (slots[:, None] < ends[None, :])
-    slot_owner = jnp.sum(jnp.where(inside, req_owner[None, :], 0), axis=1)
-    local = jnp.arange(GROUP, dtype=jnp.int32)
-    owner_of = jnp.sum(
-        jnp.where(token_lists[:, None] == group * GROUP + local[None, :], slot_owner[:, None], 0), axis=0
-    )
-    before = (owner_of[:, None] == owner_of[None, :]) & (local[:, None] < local[None, :])
-    send_slot = owner_of * SLOTS + jnp.sum(before, axis=0, dtype=jnp.int32)
-    requests = jnp.arange(req_owner.shape[0], dtype=jnp.int32)
-    own = req_owner == owner
-    own_rank = jnp.sum(own[:, None] & (requests[:, None] < requests[None, :]), axis=0)
-    padded = jnp.concatenate([token_lists, jnp.zeros((MOST + 1,), jnp.int32)])
-    held = []
-    for rank in range(REQS):
-        chosen = own & (own_rank == rank)
-        start = jnp.sum(jnp.where(chosen, starts, 0))
-        count = jnp.sum(jnp.where(chosen, req_counts, 0))
-        listed = lax.dynamic_slice(padded, (start,), (MOST,))
-        held.append(jnp.where(jnp.arange(MOST) < count, listed, -1))
-    held.append(jnp.full((ROWS - CAP,), -1, jnp.int32))
-    tokens = jnp.concatenate(held)
-    first = (tokens // GROUP) * GROUP
-    earlier = (tokens[:, None] < tokens[None, :]) & (tokens[:, None] >= first[None, :])
-    taken = jnp.sum(earlier, axis=0, dtype=jnp.int32)
-    source = jnp.where(tokens >= 0, (tokens // GROUP) * SLOTS + taken, -1)
-    return send_slot[None, :], source[:, None]
-
-
-def route_kernel(slot_ref, source_ref, merged_ref, cache_ref, packed, landed, total, send_sem, land_sem):
-    n_batch = lax.axis_size("batch")
-    me = lax.axis_index("batch")
-    barrier = pltpu.get_barrier_semaphore()
-
-    @pl.loop(1, n_batch)
-    def _(step):
-        pl.semaphore_signal(barrier, inc=1, device_id={"batch": lax.rem(me + step, n_batch)})
-
-    pl.semaphore_wait(barrier, n_batch - 1)
-
-    def copy(step):
-        return pltpu.make_async_remote_copy(
-            src_ref=packed.at[step],
-            dst_ref=landed.at[step],
-            send_sem=send_sem.at[step],
-            recv_sem=land_sem.at[step],
-            device_id={"batch": lax.rem(me + step, n_batch)},
-        )
-
-    @pl.loop(0, n_batch // PER)
-    def _(part):
-        for inner in range(PER):
-            step = part * PER + inner
-            owner = lax.rem(me + step, n_batch)
-            wanted = lax.broadcasted_iota(jnp.int32, (SLOTS, GROUP), 0) + owner * SLOTS
-            picks = jnp.where(slot_ref[...] == wanted, 1.0, 0.0).astype(jnp.bfloat16)
-            rows = jnp.dot(picks, merged_ref[...], preferred_element_type=jnp.float32)
-            packed[step] = rows.astype(jnp.bfloat16)
-        for inner in range(PER):
-            step = part * PER + inner
-
-            @pl.when(step > 0)
-            def _():
-                copy(step).start()
-
-    landed[0] = packed[0]
-
-    for part in range(n_batch // PER):
-        marks = []
-        blocks = []
-        for inner in range(PER):
-            step = part * PER + inner
-            if step > 0:
-                copy(step).wait_recv()
-            blocks.append(landed[step])
-            group = lax.rem(me - step + n_batch, n_batch)
-            marks.append(lax.broadcasted_iota(jnp.int32, (1, SLOTS), 1) + group * SLOTS)
-        marks = jnp.concatenate(marks, axis=1)
-        blocks = jnp.concatenate(blocks, axis=0)
-
-        @pl.loop(0, ROWS // 256)
-        def _(tile):
-            rows = pl.ds(pl.multiple_of(tile * 256, 256), 256)
-            picks = jnp.where(source_ref[rows, :] == marks, 1.0, 0.0).astype(jnp.bfloat16)
-            placed = jnp.dot(picks, blocks, preferred_element_type=jnp.float32)
-            if part == 0:
-                total[rows, :] = placed
-            else:
-                total[rows, :] += placed
-
-    cache_ref[...] = total[:CAP, :].astype(jnp.bfloat16)
-
-    @pl.loop(1, n_batch)
-    def _(step):
-        copy(step).wait_send()
-
-
-def route(send_slot, source, merged):
-    n_batch = lax.axis_size("batch")
-    features = merged.shape[1]
-    vmem = pl.BlockSpec(memory_space=pltpu.VMEM)
-    return pl.pallas_call(
-        route_kernel,
-        out_shape=jax.ShapeDtypeStruct((CAP, features), jnp.bfloat16),
-        in_specs=[vmem] * 3,
-        out_specs=vmem,
-        scratch_shapes=[
-            pltpu.VMEM((n_batch, SLOTS, features), jnp.bfloat16),
-            pltpu.VMEM((n_batch, SLOTS, features), jnp.bfloat16),
-            pltpu.VMEM((ROWS, features), jnp.float32),
-            pltpu.SemaphoreType.DMA((n_batch,)),
-            pltpu.SemaphoreType.DMA((n_batch,)),
-        ],
-        compiler_params=pltpu.CompilerParams(
-            collective_id=0, has_side_effects=True, vmem_limit_bytes=40 * 1024 * 1024
-        ),
-    )(send_slot, source, merged)
+    )(*arrays)
 
 
 def shards(
     patches, window_ids, norm_gain, w_qkv, b_qkv, w_proj, b_proj, merge_gain, token_lists, req_owner, req_counts
 ):
-    batch_place = lax.axis_index("batch")
-    merged = encode(
-        patches[0], window_ids, norm_gain[None], w_qkv, b_qkv, w_proj, b_proj[None], merge_gain[None]
-    )
-    send_slot, source = routing_tables(token_lists, req_owner, req_counts, batch_place, batch_place)
-    return route(send_slot, source, merged)[None]
+    return encode(
+        patches[0],
+        window_ids,
+        norm_gain.reshape(10, 128),
+        jnp.transpose(w_qkv, (0, 2, 1)).reshape(480, WIDTH),
+        b_qkv,
+        w_proj,
+        b_proj.reshape(10, 128),
+        merge_gain.reshape(10, 128),
+        token_lists.reshape(160, 128),
+        req_owner[None],
+        req_counts[None],
+    )[None]
 
 
 def solution(mesh):

time: 163 us -> 126 us (0.77)
  other arithmetic: 19.5 us -> 0 us
  local copies, waits for them, and re-layouts: 11.9 us -> 2.74 us
  between operations: 7.59 us -> 0.01 us
    reduce_sum x6 -> x0, other arithmetic: 14.6 us -> none  [the longest x1 7.96 us: routing_tables(): jnp.sum(jnp.where(token_lists[:, None] == group * GROUP + local[None, :],...]
    broadcast_in_dim x3 -> x0, local copies, waits for them, and re-layouts: 3.88 us -> none  [the longest x1 1.3 us: shards(): norm_gain[None]]
    select_n x2 -> x0, other arithmetic: 3.83 us -> none  [the longest x1 3.35 us: routing_tables(): held.append(jnp.where(jnp.arange(MOST) < count, listed, -1))]
    unnamed x4 -> x1, local copies, waits for them, and re-layouts: 5.95 us -> 2.74 us
    pallas_call x2 -> x1, Pallas kernels: 122 us -> 122 us  [encode(): pl.pallas_call(encode_kernel, out_shape=jax.ShapeDtypeStruct((CAP, GROUP)...]
where the time goes in v3:
time: 126 us; the launch traced here: 125 us
  Pallas kernels  122 us (97%)
  local copies, waits for them, and re-layouts  2.74 us (2%)
    pallas_call x1, Pallas kernels, encode(): pl.pallas_call(encode_kernel, out_shape=jax.ShapeDtypeStruct((CAP, GROUP)...  122 us
    unnamed x1, local copies, waits for them, and re-layouts  2.74 us

profile of v3, /device:TPU:27, one launch (start us, length us, event | category | flops | bytes accessed | tf_op | source)
XLA Modules:
  0.0 124.7 jit_solution(14899811155207068470)
XLA Ops:
  0.0 122.0 %shard_map.109 = bf16[1276,640]{1,0:T(8,128)(2,1)} custom-call(bf16[320,1280]{1,0:T(8,128)(2,1)} %bitcast.13, s32[1,80]{1,0:T(1,128)} %ids_ref.1, f32[10,128]{1,0:T(8,128)} %bitcast.15, bf16[480,1280]{1,0:T(8,128)(2,1)} %bitcast.12, f32[3,1280]{1,0:T(4,128)} %b_ref.1, bf16[160,1280]{1,0:T(8,128)(2,1)} %wproj_ref.1, f32[10,128]{1,0:T(8,128)} %bitcast.16, ...), custom_call_target="tpu_custom_call" | custom-call | tf_op jit(solution)/shard_map/pallas_call | solution.py:478
  122.0 2.7 %copy.13 = bf16[1,1276,640]{2,1,0:T(8,128)(2,1)} copy(bf16[1,1276,640]{2,1,0:T(8,128)(2,1)} %bitcast.11) | data formatting | bytes 3266560

commit v4 on v3

--- a/solution.py
+++ b/solution.py
@@ -121,11 +121,11 @@
 
 
 def encode_kernel(
-    patch_ref, ids_ref, gain_ref, wt, b_ref, wproj_ref, bproj_ref, merge_ref, tok_ref, owner_ref, count_ref,
+    patch_ref, ids_ref, gain_ref, w_ref, b_ref, wproj_ref, bproj_ref, merge_ref, tok_ref, owner_ref, count_ref,
     cache_ref, merged_ref, steps, jumps, owners, dests, slot, source, packed, landed, total_ref, send_sem, land_sem,
-    raw, xn, bias, q, kv, perm, id_send, id_land, id_row, id_col, attn, pieces, mixed, wp, resid,
+    raw, xn, wt, wk, bias, bias_col, bias_row, q, k, v, perm, id_send, id_land, id_row, id_col, attn, pieces, mixed, wp, resid,
     sums_out, sums_in, x_send, x_land, d_send, d_land, i_send, i_land, ws_sem, wx_sem, wy_sem,
-    a_send, a_land, f_send, f_land, s_sem,
+    a_send, a_land, f_send, f_land, s_sem, l_sem,
 ):
     place = lax.axis_index("seq")
     batch = lax.axis_index("batch")
@@ -136,6 +136,11 @@
     sibling = place + 1 - 2 * core
     right = lax.rem(x + 1, 4) * 2 + core
     left = lax.rem(x + 3, 4) * 2 + core
+    own_rows = pl.ds(pl.multiple_of(place * 320, 32), 320)
+    own_load = pltpu.make_async_copy(patch_ref, raw.at[own_rows, :], l_sem.at[0])
+    w_load = pltpu.make_async_copy(w_ref, wt, l_sem.at[1])
+    own_load.start()
+    w_load.start()
     barrier = pltpu.get_barrier_semaphore()
 
     for step in range(1, 8):
@@ -215,7 +220,6 @@
     ring(3).start()
 
     wp[own_wrows, :] = wproj_ref[:, pl.ds(pl.multiple_of(core * 640, 128), 640)]
-    raw[rows_of(x), :] = patch_ref[...]
     id_land[place] = id_send[...]
     xn[0:64, :] = jnp.zeros((64, WIDTH), jnp.bfloat16)
     xn[TALL - 64 : TALL, :] = jnp.zeros((64, WIDTH), jnp.bfloat16)
@@ -224,46 +228,56 @@
         lanes = iota((160, WIDTH), 1) == iota((160, WIDTH), 0) + place * 160
         picked = jnp.sum(jnp.where(lanes, b_ref[which : which + 1, :], 0.0), axis=1, keepdims=True)
         bias[rows, :] = jnp.broadcast_to(picked, (160, 128))
+    bias_col[...] = jnp.zeros_like(bias_col)
+    for head in range(2):
+        bias_col[head * 128 : head * 128 + 80, :] = bias[160 + head * 80 : 240 + head * 80, :]
+        flipped = jnp.transpose(bias_col[head * 128 : head * 128 + 128, :])
+        bias_row[:, head * 128 : head * 128 + 128] = flipped[0:8, :]
     inner = iota((512, 512), 1)
     perm[...] = onehot(iota((512, 512), 0) == (inner & 127) * 4 + (inner >> 7))
 
-    def project(first, count, xrow, columns, out, out_row, wide):
-        del wide
-        product = dot(wt[first : first + count, :], xn[xrow, :], ((1,), (1,)))
-        product = product + bias[first : first + count, 0:1]
-        out[out_row : out_row + count, columns] = product.astype(jnp.bfloat16)
+    def project(first, xrow, columns, out):
+        product = dot(wt[first : first + 160, :], xn[xrow, :], ((1,), (1,)))
+        out[:, columns] = (product + bias[first : first + 160, 0:1]).astype(jnp.bfloat16)
+
+    def project_keys(rows):
+        product = dot(xn[rows, :], wk[...], ((1,), (1,)))
+        k[rows, :] = (product + bias_row[0:1, :]).astype(jnp.bfloat16)
 
     def attend(block):
         own = pl.ds(pl.multiple_of(block * 128, 128), 128)
         band = pl.ds(pl.multiple_of(block * 128, 128), 256)
         matches = id_col[band, :] == id_row[0:1, own]
         for head in range(2):
-            feats = pl.ds(head * 80, 80)
-            scores = dot(kv[feats, band], q[feats, own], ((0,), (0,)))
+            feats = slice(head * 80, head * 80 + 80)
+            scores = dot(k[band, head * 128 : head * 128 + 80], q[feats, own])
             scores = jnp.where(matches, scores, -1e30)
             peak = jnp.max(scores, axis=0, keepdims=True)
             weights = jnp.exp2((scores - peak) * SCALE)
             total = jnp.sum(weights, axis=0, keepdims=True)
-            out = dot(kv[pl.ds(160 + head * 80, 80), band], weights.astype(jnp.bfloat16))
+            out = dot(v[feats, band], weights.astype(jnp.bfloat16))
             attn[feats, own] = (out * (1.0 / total)).astype(jnp.bfloat16)
+
+    def normalise(chip, halves):
+        gain = lanes_of(gain_ref, 0, 10)
+        for at in range(2):
+            for half in halves:
+                first = lax.rem(chip, 4) * 640 + at * 320 + half * 160
+
+                @pl.loop(0, 10, unroll=2)
+                def _(tile):
+                    start = pl.multiple_of(first + tile * 16, 16)
+                    rows = raw[pl.ds(start, 16), :].astype(jnp.float32)
+                    level = lax.rsqrt(jnp.mean(rows * rows, axis=1, keepdims=True) + 1e-06)
+                    xn[pl.ds(pl.multiple_of(start + 64, 16), 16), :] = (rows * level * gain).astype(jnp.bfloat16)
 
     def take_chip(chip):
         chip = lax.rem(chip, 4)
         base = chip * 640
-        gain = lanes_of(gain_ref, 0, 10)
-
-        @pl.loop(0, 10)
-        def _(tile):
-            start = pl.multiple_of(base + tile * 64, 64)
-            rows = raw[pl.ds(start, 64), :].astype(jnp.float32)
-            level = lax.rsqrt(jnp.mean(rows * rows, axis=1, keepdims=True) + 1e-06)
-            xn[pl.ds(pl.multiple_of(start + 64, 64), 64), :] = (rows * level * gain).astype(jnp.bfloat16)
-
-        project(
-            0, 160, pl.ds(pl.multiple_of(base + 64, 64), 640), pl.ds(pl.multiple_of(base, 128), 640), q, 0, 640
-        )
+        project(0, pl.ds(pl.multiple_of(base + 64, 64), 640), pl.ds(pl.multiple_of(base, 128), 640), q)
         wide = pl.ds(pl.multiple_of(base + 128, 128), 512)
-        project(160, 320, wide, wide, kv, 0, 512)
+        project_keys(wide)
+        project(320, wide, wide, v)
 
         units = jnp.concatenate([id_land[chip * 2, 0:1, :], id_land[chip * 2 + 1, 0:1, :]], axis=1)
         units = units.astype(jnp.float32).astype(jnp.bfloat16)
@@ -275,20 +289,75 @@
         id_col[pl.ds(pl.multiple_of(base + 64, 64), 640), :] = dot(
             spread, jnp.broadcast_to(units, (128, 256)), ((1,), (1,))
         )
-
-        @pl.loop(1, 4)
-        def _(tile):
+        for tile in range(1, 4):
             attend(chip * 5 + tile)
 
-    tables(tok_ref, owner_ref, count_ref, batch, steps, jumps, owners, dests, slot, source)
+    def take_edge(edge):
+        columns = pl.ds(pl.multiple_of(edge * 640, 128), 128)
+        project_keys(columns)
+        project(320, columns, columns, v)
+
+        @pl.when(edge > 0)
+        def _():
+            attend(edge * 5 - 1)
+
+        @pl.when(edge < 4)
+        def _():
+            attend(edge * 5)
+
+    def chunk_of(part):
+        return pl.ds(pl.multiple_of(part * 128, 128), 128)
+
+    def feats_of(chip, at):
+        return pl.ds(pl.multiple_of(lax.rem(chip, 4) * 320 + at * 160, 32), 160)
+
+    def a_copy(dx, part):
+        chip = lax.rem(x + dx, 4)
+        return remote(
+            pieces.at[chip, :, chunk_of(part)],
+            mixed.at[feats_of(x, core), chunk_of(part)],
+            a_send.at[dx - 1, part],
+            a_land.at[dx - 1, part],
+            seq=chip * 2 + core,
+        )
+
+    def a_share(dx, part):
+        block = mixed.at[feats_of(x + 4 - dx, core), chunk_of(part)]
+        return remote(block, block, f_send.at[dx, part], f_land.at[dx, part], seq=sibling)
+
+    def late_chip(chip):
+        return lax.rem(chip + 2, 4)
+
+    def early(chip, at):
+        return lax.rem(late_chip(chip) + 2 + at, 5)
+
+    def sort_chunk(part):
+        chunk = attn[:, pl.ds(pl.multiple_of(part * 512, 128), 512)]
+        sorted_rows = dot(chunk, perm[...]).astype(jnp.bfloat16)
+        for dest in range(4):
+            pieces[dest, :, chunk_of(part)] = sorted_rows[:, dest * 128 : dest * 128 + 128]
+        mixed[feats_of(x, core), chunk_of(part)] = pieces[x, :, chunk_of(part)]
+
+    def send_chunk(part):
+        for dx in (2, 1, 3):
+            a_copy(dx, part).start()
+        a_share(0, part).start()
+
     id_col[0:64, :] = jnp.full((64, 128), -1.0, jnp.float32)
     id_col[TALL - 64 : TALL, :] = jnp.full((64, 128), -1.0, jnp.float32)
+    w_load.wait()
+    wk[...] = jnp.zeros_like(wk)
+    for head in range(2):
+        wk[head * 128 : head * 128 + 80, :] = wt[160 + head * 80 : 240 + head * 80, :]
+    wp_swap().wait_recv()
+    for dx in range(1, 4):
+        wp_x(dx).start()
+    tables(tok_ref, owner_ref, count_ref, batch, steps, jumps, owners, dests, slot, source)
+    own_load.wait()
     for step in range(1, 8):
         id_copy(step).wait_recv()
     share(6).wait_recv()
-    wp_swap().wait_recv()
-    for dx in range(1, 4):
-        wp_x(dx).start()
+    normalise(x, (0, 1))
     take_chip(x)
     for which in (0, 1):
         ring(which).wait_recv()
@@ -298,62 +367,58 @@
         wp_x(dx).wait_recv()
         for dy in range(1, 4):
             wp_y(dx, dy).start()
+    share(0).wait_recv()
+    share(1).wait_recv()
+    normalise(x + 3, (0,))
+    normalise(x + 1, (1,))
     for which in (2, 3):
         ring(which).wait_recv()
         share(which).start()
-    share(0).wait_recv()
     share(2).wait_recv()
+    normalise(x + 3, (1,))
     take_chip(x + 3)
-    share(1).wait_recv()
     share(3).wait_recv()
+    normalise(x + 1, (0,))
     take_chip(x + 1)
+
+    @pl.loop(0, 3)
+    def _(at):
+        take_edge(early(x, at))
+
+    @pl.loop(0, 3)
+    def _(at):
+        sort_chunk(early(x, at))
+
     for which in (4, 5):
         ring(which).wait_recv()
         share(which).start()
+
+    @pl.loop(0, 3)
+    def _(at):
+        send_chunk(early(x, at))
+
     for which in (4, 5):
         share(which).wait_recv()
+    normalise(x + 2, (0, 1))
     take_chip(x + 2)
 
-    @pl.loop(0, 5)
-    def _(edge):
-        columns = pl.ds(pl.multiple_of(edge * 640, 128), 128)
-        project(160, 320, columns, columns, kv, 0, 128)
-
-    @pl.loop(0, 4)
-    def _(chip):
-        attend(chip * 5)
-        attend(chip * 5 + 4)
-
-    def chunk_of(part):
-        return pl.ds(pl.multiple_of(part * 128, 128), 128)
-
-    def feats_of(chip, at):
-        return pl.ds(pl.multiple_of(lax.rem(chip, 4) * 320 + at * 160, 32), 160)
-
-    def a_copy(dx, part):
-        chip = lax.rem(x + dx, 4)
-        return remote(
-            pieces.at[chip, :, chunk_of(part)],
-            mixed.at[feats_of(x, core), chunk_of(part)],
-            a_send.at[dx - 1, part],
-            a_land.at[dx - 1, part],
-            seq=chip * 2 + core,
-        )
-
-    def a_share(dx, part):
-        block = mixed.at[feats_of(x + 4 - dx, core), chunk_of(part)]
-        return remote(block, block, f_send.at[dx, part], f_land.at[dx, part], seq=sibling)
-
-    @pl.loop(0, 5)
-    def _(part):
-        chunk = attn[:, pl.ds(pl.multiple_of(part * 512, 128), 512)]
-        sorted_rows = dot(chunk, perm[...]).astype(jnp.bfloat16)
-        for k in range(4):
-            pieces[k, :, chunk_of(part)] = sorted_rows[:, k * 128 : k * 128 + 128]
-        for dx in (2, 1, 3):
-            a_copy(dx, part).start()
-        mixed[feats_of(x, core), chunk_of(part)] = pieces[x, :, chunk_of(part)]
-        a_share(0, part).start()
+    @pl.loop(0, 2)
+    def _(at):
+        take_edge(late_chip(x) + at)
+
+    @pl.loop(0, 2)
+    def _(at):
+        sort_chunk(late_chip(x) + at)
+        send_chunk(late_chip(x) + at)
+
+    def pass_on(dx, part):
+        a_copy(dx, part).wait_recv()
+        a_share(dx, part).start()
+
+    @pl.loop(0, 3)
+    def _(at):
+        for dx in (1, 3, 2):
+            pass_on(dx, early(x + 4 - dx, at))
 
     half = pl.ds(pl.multiple_of(core * 640, 128), 640)
     pick = onehot(iota((128, 512), 1) == iota((128, 512), 0) * 4 + x)
@@ -363,6 +428,11 @@
         rows = raw[pl.ds(pl.multiple_of(part * 512, 128), 512), half]
         resid[chunk_of(part), :] = dot(pick, rows) + lanes_of(bproj_ref, core * 5, 5)
 
+    @pl.loop(0, 2)
+    def _(at):
+        for dx in (1, 3, 2):
+            pass_on(dx, late_chip(x + 4 - dx) + at)
+
     for dx in range(1, 4):
         for dy in range(1, 4):
             wp_y(dx, dy).wait_recv()
@@ -375,9 +445,6 @@
 
     @pl.loop(0, 5)
     def _(part):
-        for dx in (1, 3, 2):
-            a_copy(dx, part).wait_recv()
-            a_share(dx, part).start()
         for dx in (0, 1, 3, 2):
             a_share(dx, part).wait_recv()
         rows = resid[chunk_of(part), :] + dot(mixed[:, chunk_of(part)], wp[...], ((0,), (0,)))
@@ -404,13 +471,11 @@
 
     @pl.loop(0, n_batch // PER)
     def _(part):
+        wanted = iota((PER * SLOTS, GROUP), 0) + (batch + part * PER) * SLOTS
+        wanted = jnp.where(wanted >= ROWS, wanted - ROWS, wanted).astype(jnp.float32)
+        rows = dot(onehot(slot[0:1, :] == wanted), merged_ref[...]).astype(jnp.bfloat16)
         for inner in range(PER):
-            step = part * PER + inner
-            owner = lax.rem(batch + step, n_batch)
-            wanted = (iota((SLOTS, GROUP), 0) + owner * SLOTS).astype(jnp.float32)
-            picks = onehot(slot[0:1, :] == wanted)
-            rows = dot(picks, merged_ref[...])
-            packed[step] = rows.astype(jnp.bfloat16)
+            packed[part * PER + inner] = rows[inner * SLOTS : inner * SLOTS + SLOTS]
         for inner in range(PER):
             step = part * PER + inner
 
@@ -420,30 +485,29 @@
 
     landed[0] = packed[0]
 
-    for part in range(n_batch // PER):
+    step = 0
+    for count in (12, 12, 6, 2):
         marks = []
         blocks = []
-        for inner in range(PER):
-            step = part * PER + inner
+        for _ in range(count):
             if step > 0:
                 copy(step).wait_recv()
             blocks.append(landed[step])
             group = lax.rem(batch - step + n_batch, n_batch)
             marks.append((iota((1, SLOTS), 1) + group * SLOTS).astype(jnp.float32))
+            step += 1
         marks = jnp.concatenate(marks, axis=1)
         blocks = jnp.concatenate(blocks, axis=0)
-
-        @pl.loop(0, ROWS // 256)
-        def _(tile):
-            rows = pl.ds(pl.multiple_of(tile * 256, 256), 256)
-            picks = onehot(source[rows, 0:1] == marks)
-            placed = dot(picks, blocks)
-            if part == 0:
+        for first in (0, GROUP):
+            rows = slice(first, first + GROUP)
+            placed = dot(onehot(source[rows, 0:1] == marks), blocks)
+            if step > count:
+                placed += total_ref[rows, :]
+            if step < 32:
                 total_ref[rows, :] = placed
             else:
-                total_ref[rows, :] += placed
-
-    cache_ref[...] = total_ref[:CAP, :].astype(jnp.bfloat16)
+                last = min(first + GROUP, CAP)
+                cache_ref[first:last, :] = placed[: last - first].astype(jnp.bfloat16)
 
     @pl.loop(1, n_batch)
     def _(step):
@@ -472,13 +536,14 @@
 
 def encode(*arrays):
     vmem = pl.BlockSpec(memory_space=pltpu.VMEM)
+    hbm = pl.BlockSpec(memory_space=pl.ANY)
     n_batch = lax.axis_size("batch")
     dma = pltpu.SemaphoreType.DMA
     bf16, f32 = jnp.bfloat16, jnp.float32
     return pl.pallas_call(
         encode_kernel,
         out_shape=jax.ShapeDtypeStruct((CAP, GROUP), bf16),
-        in_specs=[vmem] * len(arrays),
+        in_specs=[hbm, vmem, vmem, hbm] + [vmem] * (len(arrays) - 4),
         out_specs=vmem,
         scratch_shapes=[
             pltpu.VMEM((GROUP, GROUP), bf16),
@@ -494,9 +559,14 @@
             dma((n_batch,)), dma((n_batch,)),
             pltpu.VMEM((2560, WIDTH), bf16),
             pltpu.VMEM((TALL, WIDTH), bf16),
+            pltpu.VMEM((480, WIDTH), bf16),
+            pltpu.VMEM((256, WIDTH), bf16),
             pltpu.VMEM((480, 128), f32),
+            pltpu.VMEM((256, 128), f32),
+            pltpu.VMEM((8, 256), f32),
             pltpu.VMEM((160, 2560), bf16),
-            pltpu.VMEM((320, TALL), bf16),
+            pltpu.VMEM((TALL, 256), bf16),
+            pltpu.VMEM((160, TALL), bf16),
             pltpu.VMEM((512, 512), bf16),
             pltpu.VMEM((8, 128), jnp.int32),
             pltpu.VMEM((8, 8, 128), jnp.int32),
@@ -511,7 +581,7 @@
             pltpu.VMEM((GROUP, 128), f32),
             dma((6,)), dma((6,)), dma((7,)), dma((7,)), dma((8,)), dma((8,)),
             dma((2,)), dma((2, 3)), dma((2, 9)),
-            dma((3, 5)), dma((3, 5)), dma((4, 5)), dma((4, 5)), dma((2, 5)),
+            dma((3, 5)), dma((3, 5)), dma((4, 5)), dma((4, 5)), dma((2, 5)), dma((2,)),
         ],
         compiler_params=pltpu.CompilerParams(
             collective_id=0, has_side_effects=True, vmem_limit_bytes=56 * 1024 * 1024

time: 126 us -> 120 us (0.952)
  Pallas kernels: 122 us -> 115 us
    pallas_call x1, Pallas kernels: 122 us -> 115 us  [encode(): pl.pallas_call(encode_kernel, out_shape=jax.ShapeDtypeStruct((CAP, GROUP)...]
where the time goes in v4:
time: 120 us; the launch traced here: 118 us
  Pallas kernels  115 us (96%)
  local copies, waits for them, and re-layouts  2.74 us (2%)
    pallas_call x1, Pallas kernels, encode(): pl.pallas_call(encode_kernel, out_shape=jax.ShapeDtypeStruct((CAP, GROUP)...  115 us
    unnamed x1, local copies, waits for them, and re-layouts  2.74 us

profile of v4, /device:TPU:27, one launch (start us, length us, event | category | flops | bytes accessed | tf_op | source)
XLA Modules:
  0.0 118.0 jit_solution(9956434370505034622)
XLA Ops:
  0.0 115.3 %shard_map.109 = bf16[1276,640]{1,0:T(8,128)(2,1)} custom-call(bf16[320,1280]{1,0:T(8,128)(2,1)} %bitcast.13, s32[1,80]{1,0:T(1,128)} %ids_ref.1, f32[10,128]{1,0:T(8,128)} %bitcast.15, bf16[480,1280]{1,0:T(8,128)(2,1)} %bitcast.12, f32[3,1280]{1,0:T(4,128)} %b_ref.1, bf16[160,1280]{1,0:T(8,128)(2,1)} %wproj_ref.1, f32[10,128]{1,0:T(8,128)} %bitcast.16, ...), custom_call_target="tpu_custom_call" | custom-call | tf_op jit(solution)/shard_map/pallas_call | solution.py:543
  115.3 2.7 %copy.13 = bf16[1,1276,640]{2,1,0:T(8,128)(2,1)} copy(bf16[1,1276,640]{2,1,0:T(8,128)(2,1)} %bitcast.11) | data formatting | bytes 3266560

commit v5 on v4

--- a/solution.py
+++ b/solution.py
@@ -278,17 +278,6 @@
         wide = pl.ds(pl.multiple_of(base + 128, 128), 512)
         project_keys(wide)
         project(320, wide, wide, v)
-
-        units = jnp.concatenate([id_land[chip * 2, 0:1, :], id_land[chip * 2 + 1, 0:1, :]], axis=1)
-        units = units.astype(jnp.float32).astype(jnp.bfloat16)
-        spread = iota((640, 256), 0)
-        spread = onehot(jnp.where(spread < 320, spread >> 2, ((spread - 320) >> 2) + 128) == iota((640, 256), 1))
-        id_row[:, pl.ds(pl.multiple_of(base, 128), 640)] = dot(
-            jnp.broadcast_to(units, (8, 256)), spread, ((1,), (1,))
-        )
-        id_col[pl.ds(pl.multiple_of(base + 64, 64), 640), :] = dot(
-            spread, jnp.broadcast_to(units, (128, 256)), ((1,), (1,))
-        )
         for tile in range(1, 4):
             attend(chip * 5 + tile)
 
@@ -349,13 +338,19 @@
     wk[...] = jnp.zeros_like(wk)
     for head in range(2):
         wk[head * 128 : head * 128 + 80, :] = wt[160 + head * 80 : 240 + head * 80, :]
-    wp_swap().wait_recv()
-    for dx in range(1, 4):
-        wp_x(dx).start()
     tables(tok_ref, owner_ref, count_ref, batch, steps, jumps, owners, dests, slot, source)
     own_load.wait()
     for step in range(1, 8):
         id_copy(step).wait_recv()
+    spread = iota((640, 256), 0)
+    spread = onehot(jnp.where(spread < 320, spread >> 2, ((spread - 320) >> 2) + 128) == iota((640, 256), 1))
+    for chip in range(4):
+        units = jnp.concatenate([id_land[chip * 2, 0:1, :], id_land[chip * 2 + 1, 0:1, :]], axis=1)
+        units = units.astype(jnp.float32).astype(jnp.bfloat16)
+        id_row[:, chip * 640 : chip * 640 + 640] = dot(jnp.broadcast_to(units, (8, 256)), spread, ((1,), (1,)))
+        id_col[chip * 640 + 64 : chip * 640 + 704, :] = dot(
+            spread, jnp.broadcast_to(units, (128, 256)), ((1,), (1,))
+        )
     share(6).wait_recv()
     normalise(x, (0, 1))
     take_chip(x)
@@ -363,10 +358,9 @@
         ring(which).wait_recv()
         ring(which + 4).start()
         share(which).start()
+    wp_swap().wait_recv()
     for dx in range(1, 4):
-        wp_x(dx).wait_recv()
-        for dy in range(1, 4):
-            wp_y(dx, dy).start()
+        wp_x(dx).start()
     share(0).wait_recv()
     share(1).wait_recv()
     normalise(x + 3, (0,))
@@ -385,13 +379,18 @@
     def _(at):
         take_edge(early(x, at))
 
+    for which in (4, 5):
+        ring(which).wait_recv()
+        share(which).start()
+
     @pl.loop(0, 3)
     def _(at):
         sort_chunk(early(x, at))
 
-    for which in (4, 5):
-        ring(which).wait_recv()
-        share(which).start()
+    for dx in range(1, 4):
+        wp_x(dx).wait_recv()
+        for dy in range(1, 4):
+            wp_y(dx, dy).start()
 
     @pl.loop(0, 3)
     def _(at):

time: 120 us -> 114 us (0.950); the launches traced: 118 us -> 114 us
  Pallas kernels: 115 us -> 111 us
    pallas_call x1, Pallas kernels: 115 us -> 111 us  [encode(): pl.pallas_call(encode_kernel, out_shape=jax.ShapeDtypeStruct((CAP, GROUP)...]
where the time goes in v5:
time: 114 us
  Pallas kernels  111 us (97%)
  local copies, waits for them, and re-layouts  2.74 us (2%)
    pallas_call x1, Pallas kernels, encode(): pl.pallas_call(encode_kernel, out_shape=jax.ShapeDtypeStruct((CAP, GROUP)...  111 us
    unnamed x1, local copies, waits for them, and re-layouts  2.74 us

profile of v5, /device:TPU:27, one launch (start us, length us, event | category | flops | bytes accessed | tf_op | source)
XLA Modules:
  0.0 113.6 jit_solution(2461329665399353858)
XLA Ops:
  0.0 110.9 %shard_map.109 = bf16[1276,640]{1,0:T(8,128)(2,1)} custom-call(bf16[320,1280]{1,0:T(8,128)(2,1)} %bitcast.13, s32[1,80]{1,0:T(1,128)} %ids_ref.1, f32[10,128]{1,0:T(8,128)} %bitcast.15, bf16[480,1280]{1,0:T(8,128)(2,1)} %bitcast.12, f32[3,1280]{1,0:T(4,128)} %b_ref.1, bf16[160,1280]{1,0:T(8,128)(2,1)} %wproj_ref.1, f32[10,128]{1,0:T(8,128)} %bitcast.16, ...), custom_call_target="tpu_custom_call" | custom-call | tf_op jit(solution)/shard_map/pallas_call | solution.py:542
  110.9 2.7 %copy.13 = bf16[1,1276,640]{2,1,0:T(8,128)(2,1)} copy(bf16[1,1276,640]{2,1,0:T(8,128)(2,1)} %bitcast.11) | data formatting | bytes 3266560

commit v6 on v5

--- a/solution.py
+++ b/solution.py
@@ -271,20 +271,21 @@
                     level = lax.rsqrt(jnp.mean(rows * rows, axis=1, keepdims=True) + 1e-06)
                     xn[pl.ds(pl.multiple_of(start + 64, 16), 16), :] = (rows * level * gain).astype(jnp.bfloat16)
 
-    def take_chip(chip):
+    def take_chip(chip, edges=False):
         chip = lax.rem(chip, 4)
         base = chip * 640
         project(0, pl.ds(pl.multiple_of(base + 64, 64), 640), pl.ds(pl.multiple_of(base, 128), 640), q)
-        wide = pl.ds(pl.multiple_of(base + 128, 128), 512)
+        wide = pl.ds(pl.multiple_of(base, 128), 768) if edges else pl.ds(pl.multiple_of(base + 128, 128), 512)
         project_keys(wide)
         project(320, wide, wide, v)
         for tile in range(1, 4):
             attend(chip * 5 + tile)
 
-    def take_edge(edge):
-        columns = pl.ds(pl.multiple_of(edge * 640, 128), 128)
-        project_keys(columns)
-        project(320, columns, columns, v)
+    def take_edge(edge, projected=False):
+        if not projected:
+            columns = pl.ds(pl.multiple_of(edge * 640, 128), 128)
+            project_keys(columns)
+            project(320, columns, columns, v)
 
         @pl.when(edge > 0)
         def _():
@@ -340,6 +341,13 @@
         wk[head * 128 : head * 128 + 80, :] = wt[160 + head * 80 : 240 + head * 80, :]
     tables(tok_ref, owner_ref, count_ref, batch, steps, jumps, owners, dests, slot, source)
     own_load.wait()
+    for which in (0, 1):
+        ring(which).wait_recv()
+        ring(which + 4).start()
+        share(which).start()
+    wp_swap().wait_recv()
+    for dx in range(1, 4):
+        wp_x(dx).start()
     for step in range(1, 8):
         id_copy(step).wait_recv()
     spread = iota((640, 256), 0)
@@ -354,13 +362,6 @@
     share(6).wait_recv()
     normalise(x, (0, 1))
     take_chip(x)
-    for which in (0, 1):
-        ring(which).wait_recv()
-        ring(which + 4).start()
-        share(which).start()
-    wp_swap().wait_recv()
-    for dx in range(1, 4):
-        wp_x(dx).start()
     share(0).wait_recv()
     share(1).wait_recv()
     normalise(x + 3, (0,))
@@ -399,11 +400,11 @@
     for which in (4, 5):
         share(which).wait_recv()
     normalise(x + 2, (0, 1))
-    take_chip(x + 2)
+    take_chip(x + 2, True)
 
     @pl.loop(0, 2)
     def _(at):
-        take_edge(late_chip(x) + at)
+        take_edge(late_chip(x) + at, True)
 
     @pl.loop(0, 2)
     def _(at):

time: 114 us -> 113 us (level)
  no operation moved by 1% of the time
where the time goes in v6:
time: 113 us
  Pallas kernels  110 us (97%)
  local copies, waits for them, and re-layouts  2.74 us (2%)
    pallas_call x1, Pallas kernels, encode(): pl.pallas_call(encode_kernel, out_shape=jax.ShapeDtypeStruct((CAP, GROUP)...  110 us
    unnamed x1, local copies, waits for them, and re-layouts  2.74 us

profile of v6, /device:TPU:27, one launch (start us, length us, event | category | flops | bytes accessed | tf_op | source)
XLA Modules:
  0.0 112.5 jit_solution(9172708592899332144)
XLA Ops:
  0.0 109.8 %shard_map.109 = bf16[1276,640]{1,0:T(8,128)(2,1)} custom-call(bf16[320,1280]{1,0:T(8,128)(2,1)} %bitcast.13, s32[1,80]{1,0:T(1,128)} %ids_ref.1, f32[10,128]{1,0:T(8,128)} %bitcast.15, bf16[480,1280]{1,0:T(8,128)(2,1)} %bitcast.12, f32[3,1280]{1,0:T(4,128)} %b_ref.1, bf16[160,1280]{1,0:T(8,128)(2,1)} %wproj_ref.1, f32[10,128]{1,0:T(8,128)} %bitcast.16, ...), custom_call_target="tpu_custom_call" | custom-call | tf_op jit(solution)/shard_map/pallas_call | solution.py:543
  109.8 2.7 %copy.13 = bf16[1,1276,640]{2,1,0:T(8,128)(2,1)} copy(bf16[1,1276,640]{2,1,0:T(8,128)(2,1)} %bitcast.11) | data formatting | bytes 3266560

commit v7 on v6

--- a/solution.py
+++ b/solution.py
@@ -406,19 +406,19 @@
     def _(at):
         take_edge(late_chip(x) + at, True)
 
+    def pass_on(dx, part):
+        a_copy(dx, part).wait_recv()
+        a_share(dx, part).start()
+
+    @pl.loop(0, 3)
+    def _(at):
+        for dx in (1, 3, 2):
+            pass_on(dx, early(x + 4 - dx, at))
+
     @pl.loop(0, 2)
     def _(at):
         sort_chunk(late_chip(x) + at)
         send_chunk(late_chip(x) + at)
-
-    def pass_on(dx, part):
-        a_copy(dx, part).wait_recv()
-        a_share(dx, part).start()
-
-    @pl.loop(0, 3)
-    def _(at):
-        for dx in (1, 3, 2):
-            pass_on(dx, early(x + 4 - dx, at))
 
     half = pl.ds(pl.multiple_of(core * 640, 128), 640)
     pick = onehot(iota((128, 512), 1) == iota((128, 512), 0) * 4 + x)

time: 113 us -> 113 us (level)
  no operation moved by 1% of the time
where the time goes in v7:
time: 113 us
  Pallas kernels  110 us (97%)
  local copies, waits for them, and re-layouts  2.74 us (2%)
    pallas_call x1, Pallas kernels, encode(): pl.pallas_call(encode_kernel, out_shape=jax.ShapeDtypeStruct((CAP, GROUP)...  110 us
    unnamed x1, local copies, waits for them, and re-layouts  2.74 us

profile of v7, /device:TPU:27, one launch (start us, length us, event | category | flops | bytes accessed | tf_op | source)
XLA Modules:
  0.0 112.5 jit_solution(18149999018193239170)
XLA Ops:
  0.0 109.8 %shard_map.109 = bf16[1276,640]{1,0:T(8,128)(2,1)} custom-call(bf16[320,1280]{1,0:T(8,128)(2,1)} %bitcast.13, s32[1,80]{1,0:T(1,128)} %ids_ref.1, f32[10,128]{1,0:T(8,128)} %bitcast.15, bf16[480,1280]{1,0:T(8,128)(2,1)} %bitcast.12, f32[3,1280]{1,0:T(4,128)} %b_ref.1, bf16[160,1280]{1,0:T(8,128)(2,1)} %wproj_ref.1, f32[10,128]{1,0:T(8,128)} %bitcast.16, ...), custom_call_target="tpu_custom_call" | custom-call | tf_op jit(solution)/shard_map/pallas_call | solution.py:543
  109.8 2.7 %copy.13 = bf16[1,1276,640]{2,1,0:T(8,128)(2,1)} copy(bf16[1,1276,640]{2,1,0:T(8,128)(2,1)} %bitcast.11) | data formatting | bytes 3266560
